TPU v7x, 512 devices: a whole 4x4x16 slice. The times are simulated.
512 devices in a mesh: clip: 32 (over z_lo, x, core), layer: 16 (over y, z_hi).
Axes of the slice: x: 4, y: 4, z: 16 (z_hi: 4, z_lo: 4; z = z_hi * 4 + z_lo), core: 2. Of those that a mesh axis runs over, the one named last changes fastest.
Arguments:
- acts: bfloat16 [16, 8192, 5120], P('layer', 'clip'), may hold values from -6 to 6
- grads: bfloat16 [16, 8192, 5120], P('layer', 'clip'), may hold values from -6 to 6
- in_factor: bfloat16 [16, 5120, 64], P('layer'), may hold values from -0.078125 to 0.078125
- out_factor: bfloat16 [16, 5120, 64], P('layer'), may hold values from -0.078125 to 0.078125
- clip_tokens: int32 [1024], P('clip'), may hold values from 1 to 16, as said below
Outputs:
- similarity: float32 [1024, 1024], P('clip', 'layer')
Inputs may be any that keep to these rules, and one draw needn't show every extreme that they name: `clip_tokens`: the clips of every block hold exactly 256 rows together, and some clip of every block has 16 rows.
All inputs are finite; a program needn't handle non-finite values.
Results may differ from a plain program's by a relative error of at most 0.0016.
Values may be sent and summed in bfloat16 or wider, within the bound.
A program may use at most 64 MiB of HBM per device.

v0:
```python
import math

import jax
import jax.numpy as jnp
from jax import lax
from jax.sharding import PartitionSpec as P


def shifted(block, axis, distance):
    devices = range(lax.axis_size(axis))
    route = [((i - distance) % len(devices), i) for i in devices]
    return lax.ppermute(block, axis, route)


def clip_sketch(u_rows, v_rows, counts):
    row_count = u_rows.shape[1]
    starts = jnp.cumsum(counts) - counts
    position = jnp.arange(row_count, dtype=jnp.int32)
    member = (
        (position[None, :] >= starts[:, None]) & (position[None, :] < (starts + counts)[:, None])
    ).astype(jnp.bfloat16)
    masked = member[None, :, :, None] * u_rows[:, None, :, :]
    summed = jnp.einsum("lcro,lri->lcoi", masked, v_rows, preferred_element_type=jnp.float32)
    summed = summed * (1.0 / jnp.sqrt(counts.astype(jnp.float32)))[None, :, None, None]
    return summed.reshape(u_rows.shape[0], counts.shape[0], -1).astype(jnp.bfloat16)


def body(acts, grads, in_factor, out_factor, clip_tokens):
    v_rows = jnp.einsum("lrd,ldi->lri", acts, in_factor, preferred_element_type=jnp.float32).astype(
        jnp.bfloat16
    )
    u_rows = jnp.einsum(
        "lrd,ldo->lro", grads, out_factor, preferred_element_type=jnp.float32
    ).astype(jnp.bfloat16)
    own_sketch = clip_sketch(u_rows, v_rows, clip_tokens)
    clip_count = lax.axis_size("clip")
    own_index = lax.axis_index("clip")
    block_size = clip_tokens.shape[0]
    layers_all = acts.shape[0] * lax.axis_size("layer")
    norm_factor = 1.0 / math.sqrt(layers_all * in_factor.shape[2] * out_factor.shape[2])

    def advance(carried):
        return shifted(carried, "clip", -1)

    def pair_tile(other):
        return jnp.einsum("lcj,ldj->cd", own_sketch, other, preferred_element_type=jnp.float32)

    row_panel = jnp.zeros((clip_count, block_size, block_size), jnp.float32)
    row_panel = lax.dynamic_update_index_in_dim(row_panel, pair_tile(own_sketch), own_index, 0)

    def full_turn(step_index, state):
        carried, panel_now = state
        carried = advance(carried)
        tile = pair_tile(carried)
        slot = (own_index + step_index) % clip_count
        return (carried, lax.dynamic_update_index_in_dim(panel_now, tile, slot, 0))

    carried_end, row_panel = lax.fori_loop(1, clip_count, full_turn, (own_sketch, row_panel))
    rows_flat = jnp.transpose(row_panel, (1, 0, 2)).reshape(block_size, clip_count * block_size)
    summed = lax.psum_scatter(rows_flat, "layer", scatter_dimension=1, tiled=True)
    return summed * norm_factor


def solution(mesh):
    return jax.shard_map(
        body,
        mesh=mesh,
        in_specs=(
            P("layer", "clip", None),
            P("layer", "clip", None),
            P("layer", None, None),
            P("layer", None, None),
            P("clip"),
        ),
        out_specs=P("clip", "layer"),
        check_vma=False,
    )
```

profile of v0, /device:TPU:2, one launch (start us, length us, event | category | flops | bytes accessed | tf_op | source)
XLA Modules:
  0.0 555.0 jit_solution(6091233116392119264)
XLA Ops:
  17.3 399.6 %while.17 = (s32[]{:T(128)}, bf16[1,32,4096]{2,1,0:T(8,128)(2,1)}, f32[32,32,32]{2,1,0:T(8,128)}, bf16[1,32,4096]{2,1,0:T(8,128)(2,1)S(1)}, s32[]{:T(128)}, /*index=5*/s32[]{:T(128)}, s32[]{:T(128)}, s32[]{:T(128)}, s32[]{:T(128)}) while((s32[]{:T(128)}, bf16[1,32,4096]{2,1,0:T(8,128)(2,1)}, f32[32,32,32]{2,1,0:T(8,128)}, ...), condition=%wide.region_2.3_spmd, body=%wide.region_1.2_spmd.sunk | while | flops 8388625 | bytes 2113828 | solution.py:58
  24.9 5.1 collective-permute-start
  30.0 4.2 collective-permute-done
  39.4 4.2 collective-permute-done
  45.1 6.7 %collective-permute-start = (bf16[1,32,4096]{2,1,0:T(8,128)(2,1)}, bf16[1,32,4096]{2,1,0:T(8,128)(2,1)S(1)}, u32[]{:S(2)}, u32[]{:S(2)}) collective-permute-start(bf16[1,32,4096]{2,1,0:T(8,128)(2,1)} %get-tuple-element.190), channel_id=1, source_target_pairs={{16,0},{32,16},{48,32},{64,48},{80,64},{96,80},{112,96},{128,112},... | collective-permute-start | bytes 786440 | tf_op jit(solution)/shard_map/while/body/eval_jaxpr/ppermute | solution.py:12
  51.8 4.2 collective-permute-done
  57.5 7.6 %collective-permute-start = (bf16[1,32,4096]{2,1,0:T(8,128)(2,1)}, bf16[1,32,4096]{2,1,0:T(8,128)(2,1)S(1)}, u32[]{:S(2)}, u32[]{:S(2)}) collective-permute-start(bf16[1,32,4096]{2,1,0:T(8,128)(2,1)} %get-tuple-element.190), channel_id=1, source_target_pairs={{16,0},{32,16},{48,32},{64,48},{80,64},{96,80},{112,96},{128,112},... | collective-permute-start | bytes 786440 | tf_op jit(solution)/shard_map/while/body/eval_jaxpr/ppermute | solution.py:12
  70.8 7.6 %collective-permute-start = (bf16[1,32,4096]{2,1,0:T(8,128)(2,1)}, bf16[1,32,4096]{2,1,0:T(8,128)(2,1)S(1)}, u32[]{:S(2)}, u32[]{:S(2)}) collective-permute-start(bf16[1,32,4096]{2,1,0:T(8,128)(2,1)} %get-tuple-element.190), channel_id=1, source_target_pairs={{16,0},{32,16},{48,32},{64,48},{80,64},{96,80},{112,96},{128,112},... | collective-permute-start | bytes 786440 | tf_op jit(solution)/shard_map/while/body/eval_jaxpr/ppermute | solution.py:12
  78.4 4.2 collective-permute-done
  84.1 7.6 %collective-permute-start = (bf16[1,32,4096]{2,1,0:T(8,128)(2,1)}, bf16[1,32,4096]{2,1,0:T(8,128)(2,1)S(1)}, u32[]{:S(2)}, u32[]{:S(2)}) collective-permute-start(bf16[1,32,4096]{2,1,0:T(8,128)(2,1)} %get-tuple-element.190), channel_id=1, source_target_pairs={{16,0},{32,16},{48,32},{64,48},{80,64},{96,80},{112,96},{128,112},... | collective-permute-start | bytes 786440 | tf_op jit(solution)/shard_map/while/body/eval_jaxpr/ppermute | solution.py:12
  91.7 4.2 collective-permute-done
  97.4 7.6 %collective-permute-start = (bf16[1,32,4096]{2,1,0:T(8,128)(2,1)}, bf16[1,32,4096]{2,1,0:T(8,128)(2,1)S(1)}, u32[]{:S(2)}, u32[]{:S(2)}) collective-permute-start(bf16[1,32,4096]{2,1,0:T(8,128)(2,1)} %get-tuple-element.190), channel_id=1, source_target_pairs={{16,0},{32,16},{48,32},{64,48},{80,64},{96,80},{112,96},{128,112},... | collective-permute-start | bytes 786440 | tf_op jit(solution)/shard_map/while/body/eval_jaxpr/ppermute | solution.py:12
  105.1 4.2 collective-permute-done
  110.7 7.6 %collective-permute-start = (bf16[1,32,4096]{2,1,0:T(8,128)(2,1)}, bf16[1,32,4096]{2,1,0:T(8,128)(2,1)S(1)}, u32[]{:S(2)}, u32[]{:S(2)}) collective-permute-start(bf16[1,32,4096]{2,1,0:T(8,128)(2,1)} %get-tuple-element.190), channel_id=1, source_target_pairs={{16,0},{32,16},{48,32},{64,48},{80,64},{96,80},{112,96},{128,112},... | collective-permute-start | bytes 786440 | tf_op jit(solution)/shard_map/while/body/eval_jaxpr/ppermute | solution.py:12
  118.4 4.2 collective-permute-done
  124.0 7.6 %collective-permute-start = (bf16[1,32,4096]{2,1,0:T(8,128)(2,1)}, bf16[1,32,4096]{2,1,0:T(8,128)(2,1)S(1)}, u32[]{:S(2)}, u32[]{:S(2)}) collective-permute-start(bf16[1,32,4096]{2,1,0:T(8,128)(2,1)} %get-tuple-element.190), channel_id=1, source_target_pairs={{16,0},{32,16},{48,32},{64,48},{80,64},{96,80},{112,96},{128,112},... | collective-permute-start | bytes 786440 | tf_op jit(solution)/shard_map/while/body/eval_jaxpr/ppermute | solution.py:12
  131.7 4.2 collective-permute-done
  137.3 7.6 %collective-permute-start = (bf16[1,32,4096]{2,1,0:T(8,128)(2,1)}, bf16[1,32,4096]{2,1,0:T(8,128)(2,1)S(1)}, u32[]{:S(2)}, u32[]{:S(2)}) collective-permute-start(bf16[1,32,4096]{2,1,0:T(8,128)(2,1)} %get-tuple-element.190), channel_id=1, source_target_pairs={{16,0},{32,16},{48,32},{64,48},{80,64},{96,80},{112,96},{128,112},... | collective-permute-start | bytes 786440 | tf_op jit(solution)/shard_map/while/body/eval_jaxpr/ppermute | solution.py:12
  145.0 4.2 collective-permute-done
  150.7 7.6 %collective-permute-start = (bf16[1,32,4096]{2,1,0:T(8,128)(2,1)}, bf16[1,32,4096]{2,1,0:T(8,128)(2,1)S(1)}, u32[]{:S(2)}, u32[]{:S(2)}) collective-permute-start(bf16[1,32,4096]{2,1,0:T(8,128)(2,1)} %get-tuple-element.190), channel_id=1, source_target_pairs={{16,0},{32,16},{48,32},{64,48},{80,64},{96,80},{112,96},{128,112},... | collective-permute-start | bytes 786440 | tf_op jit(solution)/shard_map/while/body/eval_jaxpr/ppermute | solution.py:12
  164.0 7.6 %collective-permute-start = (bf16[1,32,4096]{2,1,0:T(8,128)(2,1)}, bf16[1,32,4096]{2,1,0:T(8,128)(2,1)S(1)}, u32[]{:S(2)}, u32[]{:S(2)}) collective-permute-start(bf16[1,32,4096]{2,1,0:T(8,128)(2,1)} %get-tuple-element.190), channel_id=1, source_target_pairs={{16,0},{32,16},{48,32},{64,48},{80,64},{96,80},{112,96},{128,112},... | collective-permute-start | bytes 786440 | tf_op jit(solution)/shard_map/while/body/eval_jaxpr/ppermute | solution.py:12
  171.6 4.2 collective-permute-done
  177.3 7.6 %collective-permute-start = (bf16[1,32,4096]{2,1,0:T(8,128)(2,1)}, bf16[1,32,4096]{2,1,0:T(8,128)(2,1)S(1)}, u32[]{:S(2)}, u32[]{:S(2)}) collective-permute-start(bf16[1,32,4096]{2,1,0:T(8,128)(2,1)} %get-tuple-element.190), channel_id=1, source_target_pairs={{16,0},{32,16},{48,32},{64,48},{80,64},{96,80},{112,96},{128,112},... | collective-permute-start | bytes 786440 | tf_op jit(solution)/shard_map/while/body/eval_jaxpr/ppermute | solution.py:12
  184.9 4.2 collective-permute-done
  190.6 7.6 %collective-permute-start = (bf16[1,32,4096]{2,1,0:T(8,128)(2,1)}, bf16[1,32,4096]{2,1,0:T(8,128)(2,1)S(1)}, u32[]{:S(2)}, u32[]{:S(2)}) collective-permute-start(bf16[1,32,4096]{2,1,0:T(8,128)(2,1)} %get-tuple-element.190), channel_id=1, source_target_pairs={{16,0},{32,16},{48,32},{64,48},{80,64},{96,80},{112,96},{128,112},... | collective-permute-start | bytes 786440 | tf_op jit(solution)/shard_map/while/body/eval_jaxpr/ppermute | solution.py:12
  198.2 4.2 collective-permute-done
  203.9 7.6 %collective-permute-start = (bf16[1,32,4096]{2,1,0:T(8,128)(2,1)}, bf16[1,32,4096]{2,1,0:T(8,128)(2,1)S(1)}, u32[]{:S(2)}, u32[]{:S(2)}) collective-permute-start(bf16[1,32,4096]{2,1,0:T(8,128)(2,1)} %get-tuple-element.190), channel_id=1, source_target_pairs={{16,0},{32,16},{48,32},{64,48},{80,64},{96,80},{112,96},{128,112},... | collective-permute-start | bytes 786440 | tf_op jit(solution)/shard_map/while/body/eval_jaxpr/ppermute | solution.py:12
  211.5 4.2 collective-permute-done
  217.2 7.6 %collective-permute-start = (bf16[1,32,4096]{2,1,0:T(8,128)(2,1)}, bf16[1,32,4096]{2,1,0:T(8,128)(2,1)S(1)}, u32[]{:S(2)}, u32[]{:S(2)}) collective-permute-start(bf16[1,32,4096]{2,1,0:T(8,128)(2,1)} %get-tuple-element.190), channel_id=1, source_target_pairs={{16,0},{32,16},{48,32},{64,48},{80,64},{96,80},{112,96},{128,112},... | collective-permute-start | bytes 786440 | tf_op jit(solution)/shard_map/while/body/eval_jaxpr/ppermute | solution.py:12
  230.5 7.6 %collective-permute-start = (bf16[1,32,4096]{2,1,0:T(8,128)(2,1)}, bf16[1,32,4096]{2,1,0:T(8,128)(2,1)S(1)}, u32[]{:S(2)}, u32[]{:S(2)}) collective-permute-start(bf16[1,32,4096]{2,1,0:T(8,128)(2,1)} %get-tuple-element.190), channel_id=1, source_target_pairs={{16,0},{32,16},{48,32},{64,48},{80,64},{96,80},{112,96},{128,112},... | collective-permute-start | bytes 786440 | tf_op jit(solution)/shard_map/while/body/eval_jaxpr/ppermute | solution.py:12
  243.8 7.6 %collective-permute-start = (bf16[1,32,4096]{2,1,0:T(8,128)(2,1)}, bf16[1,32,4096]{2,1,0:T(8,128)(2,1)S(1)}, u32[]{:S(2)}, u32[]{:S(2)}) collective-permute-start(bf16[1,32,4096]{2,1,0:T(8,128)(2,1)} %get-tuple-element.190), channel_id=1, source_target_pairs={{16,0},{32,16},{48,32},{64,48},{80,64},{96,80},{112,96},{128,112},... | collective-permute-start | bytes 786440 | tf_op jit(solution)/shard_map/while/body/eval_jaxpr/ppermute | solution.py:12
  251.5 4.2 collective-permute-done
  257.1 7.6 %collective-permute-start = (bf16[1,32,4096]{2,1,0:T(8,128)(2,1)}, bf16[1,32,4096]{2,1,0:T(8,128)(2,1)S(1)}, u32[]{:S(2)}, u32[]{:S(2)}) collective-permute-start(bf16[1,32,4096]{2,1,0:T(8,128)(2,1)} %get-tuple-element.190), channel_id=1, source_target_pairs={{16,0},{32,16},{48,32},{64,48},{80,64},{96,80},{112,96},{128,112},... | collective-permute-start | bytes 786440 | tf_op jit(solution)/shard_map/while/body/eval_jaxpr/ppermute | solution.py:12
  264.8 4.2 collective-permute-done
  270.5 7.6 %collective-permute-start = (bf16[1,32,4096]{2,1,0:T(8,128)(2,1)}, bf16[1,32,4096]{2,1,0:T(8,128)(2,1)S(1)}, u32[]{:S(2)}, u32[]{:S(2)}) collective-permute-start(bf16[1,32,4096]{2,1,0:T(8,128)(2,1)} %get-tuple-element.190), channel_id=1, source_target_pairs={{16,0},{32,16},{48,32},{64,48},{80,64},{96,80},{112,96},{128,112},... | collective-permute-start | bytes 786440 | tf_op jit(solution)/shard_map/while/body/eval_jaxpr/ppermute | solution.py:12
  278.1 4.2 collective-permute-done
  283.8 7.6 %collective-permute-start = (bf16[1,32,4096]{2,1,0:T(8,128)(2,1)}, bf16[1,32,4096]{2,1,0:T(8,128)(2,1)S(1)}, u32[]{:S(2)}, u32[]{:S(2)}) collective-permute-start(bf16[1,32,4096]{2,1,0:T(8,128)(2,1)} %get-tuple-element.190), channel_id=1, source_target_pairs={{16,0},{32,16},{48,32},{64,48},{80,64},{96,80},{112,96},{128,112},... | collective-permute-start | bytes 786440 | tf_op jit(solution)/shard_map/while/body/eval_jaxpr/ppermute | solution.py:12
  291.4 4.2 collective-permute-done
  297.1 7.6 %collective-permute-start = (bf16[1,32,4096]{2,1,0:T(8,128)(2,1)}, bf16[1,32,4096]{2,1,0:T(8,128)(2,1)S(1)}, u32[]{:S(2)}, u32[]{:S(2)}) collective-permute-start(bf16[1,32,4096]{2,1,0:T(8,128)(2,1)} %get-tuple-element.190), channel_id=1, source_target_pairs={{16,0},{32,16},{48,32},{64,48},{80,64},{96,80},{112,96},{128,112},... | collective-permute-start | bytes 786440 | tf_op jit(solution)/shard_map/while/body/eval_jaxpr/ppermute | solution.py:12
  310.4 7.6 %collective-permute-start = (bf16[1,32,4096]{2,1,0:T(8,128)(2,1)}, bf16[1,32,4096]{2,1,0:T(8,128)(2,1)S(1)}, u32[]{:S(2)}, u32[]{:S(2)}) collective-permute-start(bf16[1,32,4096]{2,1,0:T(8,128)(2,1)} %get-tuple-element.190), channel_id=1, source_target_pairs={{16,0},{32,16},{48,32},{64,48},{80,64},{96,80},{112,96},{128,112},... | collective-permute-start | bytes 786440 | tf_op jit(solution)/shard_map/while/body/eval_jaxpr/ppermute | solution.py:12
  323.7 7.6 %collective-permute-start = (bf16[1,32,4096]{2,1,0:T(8,128)(2,1)}, bf16[1,32,4096]{2,1,0:T(8,128)(2,1)S(1)}, u32[]{:S(2)}, u32[]{:S(2)}) collective-permute-start(bf16[1,32,4096]{2,1,0:T(8,128)(2,1)} %get-tuple-element.190), channel_id=1, source_target_pairs={{16,0},{32,16},{48,32},{64,48},{80,64},{96,80},{112,96},{128,112},... | collective-permute-start | bytes 786440 | tf_op jit(solution)/shard_map/while/body/eval_jaxpr/ppermute | solution.py:12
  337.0 7.6 %collective-permute-start = (bf16[1,32,4096]{2,1,0:T(8,128)(2,1)}, bf16[1,32,4096]{2,1,0:T(8,128)(2,1)S(1)}, u32[]{:S(2)}, u32[]{:S(2)}) collective-permute-start(bf16[1,32,4096]{2,1,0:T(8,128)(2,1)} %get-tuple-element.190), channel_id=1, source_target_pairs={{16,0},{32,16},{48,32},{64,48},{80,64},{96,80},{112,96},{128,112},... | collective-permute-start | bytes 786440 | tf_op jit(solution)/shard_map/while/body/eval_jaxpr/ppermute | solution.py:12
  350.3 7.6 %collective-permute-start = (bf16[1,32,4096]{2,1,0:T(8,128)(2,1)}, bf16[1,32,4096]{2,1,0:T(8,128)(2,1)S(1)}, u32[]{:S(2)}, u32[]{:S(2)}) collective-permute-start(bf16[1,32,4096]{2,1,0:T(8,128)(2,1)} %get-tuple-element.190), channel_id=1, source_target_pairs={{16,0},{32,16},{48,32},{64,48},{80,64},{96,80},{112,96},{128,112},... | collective-permute-start | bytes 786440 | tf_op jit(solution)/shard_map/while/body/eval_jaxpr/ppermute | solution.py:12
  363.6 7.6 %collective-permute-start = (bf16[1,32,4096]{2,1,0:T(8,128)(2,1)}, bf16[1,32,4096]{2,1,0:T(8,128)(2,1)S(1)}, u32[]{:S(2)}, u32[]{:S(2)}) collective-permute-start(bf16[1,32,4096]{2,1,0:T(8,128)(2,1)} %get-tuple-element.190), channel_id=1, source_target_pairs={{16,0},{32,16},{48,32},{64,48},{80,64},{96,80},{112,96},{128,112},... | collective-permute-start | bytes 786440 | tf_op jit(solution)/shard_map/while/body/eval_jaxpr/ppermute | solution.py:12
  376.9 7.6 %collective-permute-start = (bf16[1,32,4096]{2,1,0:T(8,128)(2,1)}, bf16[1,32,4096]{2,1,0:T(8,128)(2,1)S(1)}, u32[]{:S(2)}, u32[]{:S(2)}) collective-permute-start(bf16[1,32,4096]{2,1,0:T(8,128)(2,1)} %get-tuple-element.190), channel_id=1, source_target_pairs={{16,0},{32,16},{48,32},{64,48},{80,64},{96,80},{112,96},{128,112},... | collective-permute-start | bytes 786440 | tf_op jit(solution)/shard_map/while/body/eval_jaxpr/ppermute | solution.py:12
  390.2 7.6 %collective-permute-start = (bf16[1,32,4096]{2,1,0:T(8,128)(2,1)}, bf16[1,32,4096]{2,1,0:T(8,128)(2,1)S(1)}, u32[]{:S(2)}, u32[]{:S(2)}) collective-permute-start(bf16[1,32,4096]{2,1,0:T(8,128)(2,1)} %get-tuple-element.190), channel_id=1, source_target_pairs={{16,0},{32,16},{48,32},{64,48},{80,64},{96,80},{112,96},{128,112},... | collective-permute-start | bytes 786440 | tf_op jit(solution)/shard_map/while/body/eval_jaxpr/ppermute | solution.py:12
  403.6 7.6 %collective-permute-start = (bf16[1,32,4096]{2,1,0:T(8,128)(2,1)}, bf16[1,32,4096]{2,1,0:T(8,128)(2,1)S(1)}, u32[]{:S(2)}, u32[]{:S(2)}) collective-permute-start(bf16[1,32,4096]{2,1,0:T(8,128)(2,1)} %get-tuple-element.190), channel_id=1, source_target_pairs={{16,0},{32,16},{48,32},{64,48},{80,64},{96,80},{112,96},{128,112},... | collective-permute-start | bytes 786440 | tf_op jit(solution)/shard_map/while/body/eval_jaxpr/ppermute | solution.py:12
  418.9 127.8 %reduce-scatter.4.cloned.1.call-done = f32[64,32]{1,0:T(8,128)} async-done(((f32[1024,32]{1,0:T(8,128)}), f32[64,32]{1,0:T(8,128)}) %reduce-scatter.4.cloned.1.call-update) | async-done | bytes 8208
  (99 shorter events, 124.9 us)
Async XLA Ops:
  6.5 5.3 copy-start
  6.5 540.2 %reduce-scatter.4.cloned.1.call-start = ((), (), s32[]{:S(2)}) async-start(), calls=%async_computation.1 | async-start | bytes 557056
  16.5 0.8 copy-start.1
  17.3 6.1 %collective-permute-start = (bf16[1,32,4096]{2,1,0:T(8,128)(2,1)}, bf16[1,32,4096]{2,1,0:T(8,128)(2,1)S(1)}, u32[]{:S(2)}, u32[]{:S(2)}) collective-permute-start(bf16[1,32,4096]{2,1,0:T(8,128)(2,1)} %get-tuple-element.190), channel_id=1, source_target_pairs={{16,0},{32,16},{48,32},{64,48},{80,64},{96,80},{112,96},{128,112},... | collective-permute-start | bytes 786440 | tf_op jit(solution)/shard_map/while/body/eval_jaxpr/ppermute | solution.py:12
  24.9 9.3 %collective-permute-start = (bf16[1,32,4096]{2,1,0:T(8,128)(2,1)}, bf16[1,32,4096]{2,1,0:T(8,128)(2,1)S(1)}, u32[]{:S(2)}, u32[]{:S(2)}) collective-permute-start(bf16[1,32,4096]{2,1,0:T(8,128)(2,1)} %get-tuple-element.190), channel_id=1, source_target_pairs={{16,0},{32,16},{48,32},{64,48},{80,64},{96,80},{112,96},{128,112},... | collective-permute-start | bytes 786440 | tf_op jit(solution)/shard_map/while/body/eval_jaxpr/ppermute | solution.py:12
  35.7 7.9 %collective-permute-start = (bf16[1,32,4096]{2,1,0:T(8,128)(2,1)}, bf16[1,32,4096]{2,1,0:T(8,128)(2,1)S(1)}, u32[]{:S(2)}, u32[]{:S(2)}) collective-permute-start(bf16[1,32,4096]{2,1,0:T(8,128)(2,1)} %get-tuple-element.190), channel_id=1, source_target_pairs={{16,0},{32,16},{48,32},{64,48},{80,64},{96,80},{112,96},{128,112},... | collective-permute-start | bytes 786440 | tf_op jit(solution)/shard_map/while/body/eval_jaxpr/ppermute | solution.py:12
  45.1 10.9 %collective-permute-start = (bf16[1,32,4096]{2,1,0:T(8,128)(2,1)}, bf16[1,32,4096]{2,1,0:T(8,128)(2,1)S(1)}, u32[]{:S(2)}, u32[]{:S(2)}) collective-permute-start(bf16[1,32,4096]{2,1,0:T(8,128)(2,1)} %get-tuple-element.190), channel_id=1, source_target_pairs={{16,0},{32,16},{48,32},{64,48},{80,64},{96,80},{112,96},{128,112},... | collective-permute-start | bytes 786440 | tf_op jit(solution)/shard_map/while/body/eval_jaxpr/ppermute | solution.py:12
  57.5 11.8 %collective-permute-start = (bf16[1,32,4096]{2,1,0:T(8,128)(2,1)}, bf16[1,32,4096]{2,1,0:T(8,128)(2,1)S(1)}, u32[]{:S(2)}, u32[]{:S(2)}) collective-permute-start(bf16[1,32,4096]{2,1,0:T(8,128)(2,1)} %get-tuple-element.190), channel_id=1, source_target_pairs={{16,0},{32,16},{48,32},{64,48},{80,64},{96,80},{112,96},{128,112},... | collective-permute-start | bytes 786440 | tf_op jit(solution)/shard_map/while/body/eval_jaxpr/ppermute | solution.py:12
  70.8 11.8 %collective-permute-start = (bf16[1,32,4096]{2,1,0:T(8,128)(2,1)}, bf16[1,32,4096]{2,1,0:T(8,128)(2,1)S(1)}, u32[]{:S(2)}, u32[]{:S(2)}) collective-permute-start(bf16[1,32,4096]{2,1,0:T(8,128)(2,1)} %get-tuple-element.190), channel_id=1, source_target_pairs={{16,0},{32,16},{48,32},{64,48},{80,64},{96,80},{112,96},{128,112},... | collective-permute-start | bytes 786440 | tf_op jit(solution)/shard_map/while/body/eval_jaxpr/ppermute | solution.py:12
  84.1 11.8 %collective-permute-start = (bf16[1,32,4096]{2,1,0:T(8,128)(2,1)}, bf16[1,32,4096]{2,1,0:T(8,128)(2,1)S(1)}, u32[]{:S(2)}, u32[]{:S(2)}) collective-permute-start(bf16[1,32,4096]{2,1,0:T(8,128)(2,1)} %get-tuple-element.190), channel_id=1, source_target_pairs={{16,0},{32,16},{48,32},{64,48},{80,64},{96,80},{112,96},{128,112},... | collective-permute-start | bytes 786440 | tf_op jit(solution)/shard_map/while/body/eval_jaxpr/ppermute | solution.py:12
  97.4 11.8 %collective-permute-start = (bf16[1,32,4096]{2,1,0:T(8,128)(2,1)}, bf16[1,32,4096]{2,1,0:T(8,128)(2,1)S(1)}, u32[]{:S(2)}, u32[]{:S(2)}) collective-permute-start(bf16[1,32,4096]{2,1,0:T(8,128)(2,1)} %get-tuple-element.190), channel_id=1, source_target_pairs={{16,0},{32,16},{48,32},{64,48},{80,64},{96,80},{112,96},{128,112},... | collective-permute-start | bytes 786440 | tf_op jit(solution)/shard_map/while/body/eval_jaxpr/ppermute | solution.py:12
  110.7 11.8 %collective-permute-start = (bf16[1,32,4096]{2,1,0:T(8,128)(2,1)}, bf16[1,32,4096]{2,1,0:T(8,128)(2,1)S(1)}, u32[]{:S(2)}, u32[]{:S(2)}) collective-permute-start(bf16[1,32,4096]{2,1,0:T(8,128)(2,1)} %get-tuple-element.190), channel_id=1, source_target_pairs={{16,0},{32,16},{48,32},{64,48},{80,64},{96,80},{112,96},{128,112},... | collective-permute-start | bytes 786440 | tf_op jit(solution)/shard_map/while/body/eval_jaxpr/ppermute | solution.py:12
  124.0 11.8 %collective-permute-start = (bf16[1,32,4096]{2,1,0:T(8,128)(2,1)}, bf16[1,32,4096]{2,1,0:T(8,128)(2,1)S(1)}, u32[]{:S(2)}, u32[]{:S(2)}) collective-permute-start(bf16[1,32,4096]{2,1,0:T(8,128)(2,1)} %get-tuple-element.190), channel_id=1, source_target_pairs={{16,0},{32,16},{48,32},{64,48},{80,64},{96,80},{112,96},{128,112},... | collective-permute-start | bytes 786440 | tf_op jit(solution)/shard_map/while/body/eval_jaxpr/ppermute | solution.py:12
  137.3 11.8 %collective-permute-start = (bf16[1,32,4096]{2,1,0:T(8,128)(2,1)}, bf16[1,32,4096]{2,1,0:T(8,128)(2,1)S(1)}, u32[]{:S(2)}, u32[]{:S(2)}) collective-permute-start(bf16[1,32,4096]{2,1,0:T(8,128)(2,1)} %get-tuple-element.190), channel_id=1, source_target_pairs={{16,0},{32,16},{48,32},{64,48},{80,64},{96,80},{112,96},{128,112},... | collective-permute-start | bytes 786440 | tf_op jit(solution)/shard_map/while/body/eval_jaxpr/ppermute | solution.py:12
  150.7 11.8 %collective-permute-start = (bf16[1,32,4096]{2,1,0:T(8,128)(2,1)}, bf16[1,32,4096]{2,1,0:T(8,128)(2,1)S(1)}, u32[]{:S(2)}, u32[]{:S(2)}) collective-permute-start(bf16[1,32,4096]{2,1,0:T(8,128)(2,1)} %get-tuple-element.190), channel_id=1, source_target_pairs={{16,0},{32,16},{48,32},{64,48},{80,64},{96,80},{112,96},{128,112},... | collective-permute-start | bytes 786440 | tf_op jit(solution)/shard_map/while/body/eval_jaxpr/ppermute | solution.py:12
  164.0 11.8 %collective-permute-start = (bf16[1,32,4096]{2,1,0:T(8,128)(2,1)}, bf16[1,32,4096]{2,1,0:T(8,128)(2,1)S(1)}, u32[]{:S(2)}, u32[]{:S(2)}) collective-permute-start(bf16[1,32,4096]{2,1,0:T(8,128)(2,1)} %get-tuple-element.190), channel_id=1, source_target_pairs={{16,0},{32,16},{48,32},{64,48},{80,64},{96,80},{112,96},{128,112},... | collective-permute-start | bytes 786440 | tf_op jit(solution)/shard_map/while/body/eval_jaxpr/ppermute | solution.py:12
  177.3 11.8 %collective-permute-start = (bf16[1,32,4096]{2,1,0:T(8,128)(2,1)}, bf16[1,32,4096]{2,1,0:T(8,128)(2,1)S(1)}, u32[]{:S(2)}, u32[]{:S(2)}) collective-permute-start(bf16[1,32,4096]{2,1,0:T(8,128)(2,1)} %get-tuple-element.190), channel_id=1, source_target_pairs={{16,0},{32,16},{48,32},{64,48},{80,64},{96,80},{112,96},{128,112},... | collective-permute-start | bytes 786440 | tf_op jit(solution)/shard_map/while/body/eval_jaxpr/ppermute | solution.py:12
  190.6 11.8 %collective-permute-start = (bf16[1,32,4096]{2,1,0:T(8,128)(2,1)}, bf16[1,32,4096]{2,1,0:T(8,128)(2,1)S(1)}, u32[]{:S(2)}, u32[]{:S(2)}) collective-permute-start(bf16[1,32,4096]{2,1,0:T(8,128)(2,1)} %get-tuple-element.190), channel_id=1, source_target_pairs={{16,0},{32,16},{48,32},{64,48},{80,64},{96,80},{112,96},{128,112},... | collective-permute-start | bytes 786440 | tf_op jit(solution)/shard_map/while/body/eval_jaxpr/ppermute | solution.py:12
  203.9 11.8 %collective-permute-start = (bf16[1,32,4096]{2,1,0:T(8,128)(2,1)}, bf16[1,32,4096]{2,1,0:T(8,128)(2,1)S(1)}, u32[]{:S(2)}, u32[]{:S(2)}) collective-permute-start(bf16[1,32,4096]{2,1,0:T(8,128)(2,1)} %get-tuple-element.190), channel_id=1, source_target_pairs={{16,0},{32,16},{48,32},{64,48},{80,64},{96,80},{112,96},{128,112},... | collective-permute-start | bytes 786440 | tf_op jit(solution)/shard_map/while/body/eval_jaxpr/ppermute | solution.py:12
  217.2 11.8 %collective-permute-start = (bf16[1,32,4096]{2,1,0:T(8,128)(2,1)}, bf16[1,32,4096]{2,1,0:T(8,128)(2,1)S(1)}, u32[]{:S(2)}, u32[]{:S(2)}) collective-permute-start(bf16[1,32,4096]{2,1,0:T(8,128)(2,1)} %get-tuple-element.190), channel_id=1, source_target_pairs={{16,0},{32,16},{48,32},{64,48},{80,64},{96,80},{112,96},{128,112},... | collective-permute-start | bytes 786440 | tf_op jit(solution)/shard_map/while/body/eval_jaxpr/ppermute | solution.py:12
  230.5 11.8 %collective-permute-start = (bf16[1,32,4096]{2,1,0:T(8,128)(2,1)}, bf16[1,32,4096]{2,1,0:T(8,128)(2,1)S(1)}, u32[]{:S(2)}, u32[]{:S(2)}) collective-permute-start(bf16[1,32,4096]{2,1,0:T(8,128)(2,1)} %get-tuple-element.190), channel_id=1, source_target_pairs={{16,0},{32,16},{48,32},{64,48},{80,64},{96,80},{112,96},{128,112},... | collective-permute-start | bytes 786440 | tf_op jit(solution)/shard_map/while/body/eval_jaxpr/ppermute | solution.py:12
  243.8 11.8 %collective-permute-start = (bf16[1,32,4096]{2,1,0:T(8,128)(2,1)}, bf16[1,32,4096]{2,1,0:T(8,128)(2,1)S(1)}, u32[]{:S(2)}, u32[]{:S(2)}) collective-permute-start(bf16[1,32,4096]{2,1,0:T(8,128)(2,1)} %get-tuple-element.190), channel_id=1, source_target_pairs={{16,0},{32,16},{48,32},{64,48},{80,64},{96,80},{112,96},{128,112},... | collective-permute-start | bytes 786440 | tf_op jit(solution)/shard_map/while/body/eval_jaxpr/ppermute | solution.py:12
  257.1 11.8 %collective-permute-start = (bf16[1,32,4096]{2,1,0:T(8,128)(2,1)}, bf16[1,32,4096]{2,1,0:T(8,128)(2,1)S(1)}, u32[]{:S(2)}, u32[]{:S(2)}) collective-permute-start(bf16[1,32,4096]{2,1,0:T(8,128)(2,1)} %get-tuple-element.190), channel_id=1, source_target_pairs={{16,0},{32,16},{48,32},{64,48},{80,64},{96,80},{112,96},{128,112},... | collective-permute-start | bytes 786440 | tf_op jit(solution)/shard_map/while/body/eval_jaxpr/ppermute | solution.py:12
  270.5 11.8 %collective-permute-start = (bf16[1,32,4096]{2,1,0:T(8,128)(2,1)}, bf16[1,32,4096]{2,1,0:T(8,128)(2,1)S(1)}, u32[]{:S(2)}, u32[]{:S(2)}) collective-permute-start(bf16[1,32,4096]{2,1,0:T(8,128)(2,1)} %get-tuple-element.190), channel_id=1, source_target_pairs={{16,0},{32,16},{48,32},{64,48},{80,64},{96,80},{112,96},{128,112},... | collective-permute-start | bytes 786440 | tf_op jit(solution)/shard_map/while/body/eval_jaxpr/ppermute | solution.py:12
  283.8 11.8 %collective-permute-start = (bf16[1,32,4096]{2,1,0:T(8,128)(2,1)}, bf16[1,32,4096]{2,1,0:T(8,128)(2,1)S(1)}, u32[]{:S(2)}, u32[]{:S(2)}) collective-permute-start(bf16[1,32,4096]{2,1,0:T(8,128)(2,1)} %get-tuple-element.190), channel_id=1, source_target_pairs={{16,0},{32,16},{48,32},{64,48},{80,64},{96,80},{112,96},{128,112},... | collective-permute-start | bytes 786440 | tf_op jit(solution)/shard_map/while/body/eval_jaxpr/ppermute | solution.py:12
  297.1 11.8 %collective-permute-start = (bf16[1,32,4096]{2,1,0:T(8,128)(2,1)}, bf16[1,32,4096]{2,1,0:T(8,128)(2,1)S(1)}, u32[]{:S(2)}, u32[]{:S(2)}) collective-permute-start(bf16[1,32,4096]{2,1,0:T(8,128)(2,1)} %get-tuple-element.190), channel_id=1, source_target_pairs={{16,0},{32,16},{48,32},{64,48},{80,64},{96,80},{112,96},{128,112},... | collective-permute-start | bytes 786440 | tf_op jit(solution)/shard_map/while/body/eval_jaxpr/ppermute | solution.py:12
  310.4 11.8 %collective-permute-start = (bf16[1,32,4096]{2,1,0:T(8,128)(2,1)}, bf16[1,32,4096]{2,1,0:T(8,128)(2,1)S(1)}, u32[]{:S(2)}, u32[]{:S(2)}) collective-permute-start(bf16[1,32,4096]{2,1,0:T(8,128)(2,1)} %get-tuple-element.190), channel_id=1, source_target_pairs={{16,0},{32,16},{48,32},{64,48},{80,64},{96,80},{112,96},{128,112},... | collective-permute-start | bytes 786440 | tf_op jit(solution)/shard_map/while/body/eval_jaxpr/ppermute | solution.py:12
  323.7 11.8 %collective-permute-start = (bf16[1,32,4096]{2,1,0:T(8,128)(2,1)}, bf16[1,32,4096]{2,1,0:T(8,128)(2,1)S(1)}, u32[]{:S(2)}, u32[]{:S(2)}) collective-permute-start(bf16[1,32,4096]{2,1,0:T(8,128)(2,1)} %get-tuple-element.190), channel_id=1, source_target_pairs={{16,0},{32,16},{48,32},{64,48},{80,64},{96,80},{112,96},{128,112},... | collective-permute-start | bytes 786440 | tf_op jit(solution)/shard_map/while/body/eval_jaxpr/ppermute | solution.py:12
  337.0 11.8 %collective-permute-start = (bf16[1,32,4096]{2,1,0:T(8,128)(2,1)}, bf16[1,32,4096]{2,1,0:T(8,128)(2,1)S(1)}, u32[]{:S(2)}, u32[]{:S(2)}) collective-permute-start(bf16[1,32,4096]{2,1,0:T(8,128)(2,1)} %get-tuple-element.190), channel_id=1, source_target_pairs={{16,0},{32,16},{48,32},{64,48},{80,64},{96,80},{112,96},{128,112},... | collective-permute-start | bytes 786440 | tf_op jit(solution)/shard_map/while/body/eval_jaxpr/ppermute | solution.py:12
  350.3 11.8 %collective-permute-start = (bf16[1,32,4096]{2,1,0:T(8,128)(2,1)}, bf16[1,32,4096]{2,1,0:T(8,128)(2,1)S(1)}, u32[]{:S(2)}, u32[]{:S(2)}) collective-permute-start(bf16[1,32,4096]{2,1,0:T(8,128)(2,1)} %get-tuple-element.190), channel_id=1, source_target_pairs={{16,0},{32,16},{48,32},{64,48},{80,64},{96,80},{112,96},{128,112},... | collective-permute-start | bytes 786440 | tf_op jit(solution)/shard_map/while/body/eval_jaxpr/ppermute | solution.py:12
  363.6 11.8 %collective-permute-start = (bf16[1,32,4096]{2,1,0:T(8,128)(2,1)}, bf16[1,32,4096]{2,1,0:T(8,128)(2,1)S(1)}, u32[]{:S(2)}, u32[]{:S(2)}) collective-permute-start(bf16[1,32,4096]{2,1,0:T(8,128)(2,1)} %get-tuple-element.190), channel_id=1, source_target_pairs={{16,0},{32,16},{48,32},{64,48},{80,64},{96,80},{112,96},{128,112},... | collective-permute-start | bytes 786440 | tf_op jit(solution)/shard_map/while/body/eval_jaxpr/ppermute | solution.py:12
  376.9 11.8 %collective-permute-start = (bf16[1,32,4096]{2,1,0:T(8,128)(2,1)}, bf16[1,32,4096]{2,1,0:T(8,128)(2,1)S(1)}, u32[]{:S(2)}, u32[]{:S(2)}) collective-permute-start(bf16[1,32,4096]{2,1,0:T(8,128)(2,1)} %get-tuple-element.190), channel_id=1, source_target_pairs={{16,0},{32,16},{48,32},{64,48},{80,64},{96,80},{112,96},{128,112},... | collective-permute-start | bytes 786440 | tf_op jit(solution)/shard_map/while/body/eval_jaxpr/ppermute | solution.py:12
  390.2 11.8 %collective-permute-start = (bf16[1,32,4096]{2,1,0:T(8,128)(2,1)}, bf16[1,32,4096]{2,1,0:T(8,128)(2,1)S(1)}, u32[]{:S(2)}, u32[]{:S(2)}) collective-permute-start(bf16[1,32,4096]{2,1,0:T(8,128)(2,1)} %get-tuple-element.190), channel_id=1, source_target_pairs={{16,0},{32,16},{48,32},{64,48},{80,64},{96,80},{112,96},{128,112},... | collective-permute-start | bytes 786440 | tf_op jit(solution)/shard_map/while/body/eval_jaxpr/ppermute | solution.py:12
  403.6 11.8 %collective-permute-start = (bf16[1,32,4096]{2,1,0:T(8,128)(2,1)}, bf16[1,32,4096]{2,1,0:T(8,128)(2,1)S(1)}, u32[]{:S(2)}, u32[]{:S(2)}) collective-permute-start(bf16[1,32,4096]{2,1,0:T(8,128)(2,1)} %get-tuple-element.190), channel_id=1, source_target_pairs={{16,0},{32,16},{48,32},{64,48},{80,64},{96,80},{112,96},{128,112},... | collective-permute-start | bytes 786440 | tf_op jit(solution)/shard_map/while/body/eval_jaxpr/ppermute | solution.py:12
Sparse Core Ops, SparseCore 0:
  419.1 127.6 reduce-scatter.3
where the time goes:
time: 560 us; the launch traced here: 555 us
  waiting for transfers between devices  257 us (46%)
  starting transfers between devices  223 us (40%)
  matrix products  31.4 us (6%)
  local copies, waits for them, and re-layouts  27.4 us (5%)
  between operations  13.4 us (2%)
    ppermute x31, starting transfers between devices, shifted(): return lax.ppermute(block, axis, route)  223 us
    ppermute x31, waiting for transfers between devices, shifted(): return lax.ppermute(block, axis, route)  129 us
    unnamed x2, waiting for transfers between devices  128 us
    dot_general x32, matrix products, pair_tile(): jnp.einsum('lcj,ldj->cd', own_sketch, other, preferred_element_type=jnp.f...  25.8 us
    while x31, local copies, waits for them, and re-layouts  21.7 us
  transfers between devices with their start and end apart: 32, of which 32 were waited for; matrix products, arithmetic and copies ran while one was open for 0% of the time, Pallas kernels for 0%

commit v1 on v0

v1 whole, which is shorter than its diff:
```python
import functools
import math

import jax
import jax.numpy as jnp
from jax import lax
from jax.experimental import pallas as pl
from jax.experimental.pallas import tpu as pltpu
from jax.sharding import PartitionSpec as P

MESH = pl.DeviceIdType.MESH
NT = (((1,), (1,)), ((), ()))
ROWS = 256
CLIPS = 32
WIDE = 64
IDS = 16
PIECES = 4


def dot_nt(a, b):
    return lax.dot_general(a, b, NT, preferred_element_type=jnp.float32)


def inverse_root(n):
    r = lax.rsqrt(n)
    return r * (1.5 - 0.5 * n * r * r)


def kernel(
    acts, grads, in_t, out_t, tokens, out,
    abuf, gbuf, ibuf, obuf, blocks, pool_r, pool_c, scale_r, scale_c,
    part, near, half, far,
    load_sem, send1, recv1, send2, recv2, send3, recv3,
):
    clip, layer = lax.axis_index("clip"), lax.axis_index("layer")
    z, x, core = clip // 8, (clip // 2) % 4, clip % 2
    y, zh = layer // 4, layer % 4

    def at(clip_bits, layer_bits):
        return (jnp.bitwise_xor(clip, clip_bits), jnp.bitwise_xor(layer, layer_bits))

    loads = [
        pltpu.make_async_copy(in_t.at[0], ibuf, load_sem.at[0]),
        pltpu.make_async_copy(out_t.at[0], obuf, load_sem.at[1]),
    ]
    step = ROWS // PIECES
    for i in range(PIECES):
        rows = pl.ds(i * step, step)
        loads.append(pltpu.make_async_copy(acts.at[0, rows], abuf.at[rows], load_sem.at[2 + 2 * i]))
        loads.append(pltpu.make_async_copy(grads.at[0, rows], gbuf.at[rows], load_sem.at[3 + 2 * i]))
    for load in loads:
        load.start()

    peers = [(1, 0)]
    peers += [(8 * d, 0) for d in range(1, 4)]
    peers += [(2 * dx, 4 * dy) for dx in range(4) for dy in range(4) if dx or dy]
    peers += [(0, d) for d in range(1, 4)]
    barrier = pltpu.get_barrier_semaphore()
    for bits in peers:
        pl.semaphore_signal(barrier, inc=1, device_id=at(*bits), device_id_type=MESH)

    place = lax.broadcasted_iota(jnp.int32, (IDS, 128), 0) * 128 + lax.broadcasted_iota(
        jnp.int32, (IDS, 128), 1
    )
    owner = jnp.zeros((IDS, 128), jnp.int32)
    end = jnp.int32(0)
    for c in range(CLIPS - 1):
        end = end + tokens[c]
        owner = owner + jnp.where(place >= end, 1, 0)
    blocks[0, ROWS:, :] = owner.astype(jnp.float32).astype(jnp.bfloat16)

    loads[0].wait()
    loads[1].wait()
    for i in range(PIECES):
        rows = pl.ds(i * step, step)
        loads[2 + 2 * i].wait()
        loads[3 + 2 * i].wait()
        v = dot_nt(abuf[rows, :], ibuf[...])
        u = dot_nt(gbuf[rows, :], obuf[...])
        blocks[0, rows, :] = jnp.concatenate([u, v], axis=1).astype(jnp.bfloat16)

    pl.semaphore_wait(barrier, len(peers))

    def send_block(src, dst, bits):
        copy = pltpu.make_async_remote_copy(
            src_ref=blocks.at[src], dst_ref=blocks.at[dst], send_sem=send1.at[dst],
            recv_sem=recv1.at[dst], device_id=at(bits, 0), device_id_type=MESH,
        )
        copy.start()
        return copy

    copies = {}
    for d in (3, 2, 1):
        copies[4 + d] = send_block(0, 4 + d, 8 * d)
    copies[4] = send_block(0, 4, 1)
    for d in (2, 1, 3):
        copies[d] = send_block(0, d, 2 * d)

    lane = lax.broadcasted_iota(jnp.int32, (1, 128), 1)

    def row_pool(slot):
        ids = blocks[slot, ROWS:, :].astype(jnp.float32)
        which = lax.broadcasted_iota(jnp.int32, (CLIPS, 128), 0).astype(jnp.float32)
        hot = jnp.concatenate(
            [jnp.where(which == ids[i : i + 1, :], 1.0, 0.0) for i in range(2)], axis=1
        )
        pool_r[slot] = hot.astype(jnp.bfloat16)
        scale = inverse_root(jnp.sum(hot, axis=1, keepdims=True))
        scale_r[slot] = jnp.where(lane < 64, scale[0:16], scale[16:32])

    def col_pool(slot, side):
        ids = blocks[slot, ROWS:, :].astype(jnp.float32)
        j = lax.broadcasted_iota(jnp.int32, (128, 128), 0)
        which = jnp.where((j // CLIPS) % 2 == side, j % CLIPS, -1).astype(jnp.float32)
        hot = jnp.concatenate(
            [jnp.where(which == ids[i : i + 1, :], 1.0, 0.0) for i in range(2)], axis=1
        ).astype(jnp.bfloat16)
        return hot

    def unit(dx, dz, same, other):
        rows = blocks[dx, pl.ds(0, ROWS), :]
        row_u = jnp.where(lane < WIDE, rows, jnp.zeros_like(rows))
        row_v = jnp.where(lane < WIDE, jnp.zeros_like(rows), rows)
        pooled = jnp.zeros((ROWS, 128), jnp.float32)
        for k, slot in enumerate((same, other)):
            cols = blocks[slot, 0:ROWS, :]
            gram = (dot_nt(row_u, cols) * dot_nt(row_v, cols)).astype(jnp.bfloat16)
            pooled = pooled + dot_nt(gram, pool_c[dz, k])
        tile = jnp.dot(pool_r[dx], pooled.astype(jnp.bfloat16), preferred_element_type=jnp.float32)
        packed = jnp.where(lane < 64, tile[0:16], tile[16:32])
        return packed * scale_r[dx] * scale_c[dz, 0:1, :]

    def to_near(dx, dz):
        dy = jnp.bitwise_xor(jnp.bitwise_xor(y, z), dz)
        slot = dx * 4 + dy
        copy = pltpu.make_async_remote_copy(
            src_ref=part.at[dz, dx], dst_ref=near.at[slot], send_sem=send2.at[dz * 4 + dx],
            recv_sem=recv2.at[slot], device_id=at(2 * dx, 4 * dy), device_id_type=MESH,
        )
        return slot, copy

    for dz in range(4):
        same, other = (0, 4) if dz == 0 else (4 + dz, 7 + dz)
        if dz:
            copies[same].wait_recv()
            copies[other] = send_block(same, other, 1)
        copies[other].wait_recv()
        for k, slot in enumerate((same, other)):
            pool_c[dz, k] = col_pool(slot, core if k == 0 else 1 - core)
        counts = sum(dot_nt(jnp.ones((16, ROWS), jnp.bfloat16), pool_c[dz, k]) for k in range(2))
        scale_c[dz] = inverse_root(counts)
        if dz == 0:
            row_pool(0)

        for dx in range(4):
            if dz == 0 and dx:
                copies[dx].wait_recv()
                row_pool(dx)
            part[dz, dx] = unit(dx, dz, same, other)
            slot, copy = to_near(dx, dz)
            if dx:
                copy.start()
            else:

                @pl.when(slot != 0)
                def _():
                    copy.start()

                @pl.when(slot == 0)
                def _():
                    near[0] = part[dz, 0]

    def gathered(d):
        dx = jnp.bitwise_xor(jnp.bitwise_xor(x, zh), d)
        total = jnp.zeros((16, 128), jnp.float32)
        for dy in range(4):
            slot = dx * 4 + dy
            arrival = pltpu.make_async_remote_copy(
                src_ref=part.at[0, 0], dst_ref=near.at[slot], send_sem=send2.at[0],
                recv_sem=recv2.at[slot], device_id=at(1, 0), device_id_type=MESH,
            )
            if dy:
                arrival.wait_recv()
            else:

                @pl.when(slot != 0)
                def _():
                    arrival.wait_recv()

            total = total + near[slot]
        return total

    last = []
    for d in (2, 1, 3):
        half[d] = gathered(d)
        copy = pltpu.make_async_remote_copy(
            src_ref=half.at[d], dst_ref=far.at[d], send_sem=send3.at[d], recv_sem=recv3.at[d],
            device_id=at(0, d), device_id_type=MESH,
        )
        copy.start()
        last.append(copy)
    total = gathered(0)
    for copy, d in zip(last, (2, 1, 3), strict=True):
        copy.wait_recv()
        total = total + far[d]
    total = total * (1.0 / math.sqrt(16 * WIDE * WIDE))
    out[0:16, :] = total[:, 0:64]
    out[16:32, :] = total[:, 64:128]

    for copy in copies.values():
        copy.wait_send()
    for dz in range(4):
        for dx in range(4):
            slot, copy = to_near(dx, dz)
            if dx:
                copy.wait_send()
            else:

                @pl.when(slot != 0)
                def _():
                    copy.wait_send()

    for copy in last:
        copy.wait_send()


def body(acts, grads, in_factor, out_factor, clip_tokens):
    depth = acts.shape[2]
    bf16, f32 = jnp.bfloat16, jnp.float32
    hbm = pl.BlockSpec(memory_space=pltpu.HBM)
    return pl.pallas_call(
        kernel,
        out_shape=jax.ShapeDtypeStruct((CLIPS, 64), f32),
        in_specs=[hbm] * 4 + [pl.BlockSpec(memory_space=pltpu.SMEM)],
        out_specs=pl.BlockSpec(memory_space=pltpu.VMEM),
        scratch_shapes=[
            pltpu.VMEM((ROWS, depth), bf16),
            pltpu.VMEM((ROWS, depth), bf16),
            pltpu.VMEM((WIDE, depth), bf16),
            pltpu.VMEM((WIDE, depth), bf16),
            pltpu.VMEM((11, ROWS + IDS, 128), bf16),
            pltpu.VMEM((4, CLIPS, ROWS), bf16),
            pltpu.VMEM((4, 2, 128, ROWS), bf16),
            pltpu.VMEM((4, 16, 128), f32),
            pltpu.VMEM((4, 16, 128), f32),
            pltpu.VMEM((4, 4, 16, 128), f32),
            pltpu.VMEM((16, 16, 128), f32),
            pltpu.VMEM((4, 16, 128), f32),
            pltpu.VMEM((4, 16, 128), f32),
            pltpu.SemaphoreType.DMA((2 + 2 * PIECES,)),
            pltpu.SemaphoreType.DMA((11,)),
            pltpu.SemaphoreType.DMA((11,)),
            pltpu.SemaphoreType.DMA((16,)),
            pltpu.SemaphoreType.DMA((16,)),
            pltpu.SemaphoreType.DMA((4,)),
            pltpu.SemaphoreType.DMA((4,)),
        ],
        compiler_params=pltpu.CompilerParams(
            collective_id=0, has_side_effects=True, vmem_limit_bytes=60 * 1024 * 1024
        ),
        cost_estimate=pl.CostEstimate(flops=10**9, bytes_accessed=7 * 10**6, transcendentals=0),
        name="similarity",
    )(
        acts,
        grads,
        jnp.swapaxes(in_factor, 1, 2),
        jnp.swapaxes(out_factor, 1, 2),
        clip_tokens,
    )


def solution(mesh):
    return jax.shard_map(
        body,
        mesh=mesh,
        in_specs=(
            P("layer", "clip", None),
            P("layer", "clip", None),
            P("layer", None, None),
            P("layer", None, None),
            P("clip"),
        ),
        out_specs=P("clip", "layer"),
        check_vma=False,
    )
```

time: 560 us -> 43.7 us (0.08)
  the two profiles are of different devices: /device:TPU:2 before, /device:TPU:30 now
where the time goes in v1:
time: 43.7 us; the launch traced here: 43.5 us
  Pallas kernels  42.2 us (97%)
  local copies, waits for them, and re-layouts  1.32 us (3%)
    pallas_call x1, Pallas kernels, body(): pl.pallas_call(kernel, out_shape=jax.ShapeDtypeStruct((CLIPS, 64), f32),...  42.2 us
    unnamed x1, local copies, waits for them, and re-layouts  1.32 us

profile of v1, /device:TPU:30, one launch (start us, length us, event | category | flops | bytes accessed | tf_op | source)
XLA Modules:
  0.0 43.5 jit_solution(6513123484781951275)
XLA Ops:
  0.0 42.2 %similarity.1 = f32[32,64]{1,0:T(8,128)} custom-call(bf16[1,256,5120]{2,1,0:T(8,128)(2,1)} %acts.1, bf16[1,256,5120]{2,1,0:T(8,128)(2,1)} %grads.1, bf16[1,64,5120]{2,1,0:T(8,128)(2,1)} %bitcast.2, bf16[1,64,5120]{2,1,0:T(8,128)(2,1)} %bitcast.3, s32[32]{0:T(128)} %tokens.1), custom_call_target="tpu_custom_call" | custom-call | flops 1000000000 | bytes 7000000 | tf_op jit(solution)/shard_map/similarity/pallas_call | solution.py:231
  42.2 1.3 %copy.7 = f32[32,64]{1,0:T(8,128)} copy(f32[32,64]{1,0:T(8,128)} %similarity.1) | data formatting | bytes 16384

commit v2 on v1

v2 whole, which is shorter than its diff:
```python
import functools
import math

import jax
import jax.numpy as jnp
from jax import lax
from jax.experimental import pallas as pl
from jax.experimental.pallas import tpu as pltpu
from jax.sharding import PartitionSpec as P

MESH = pl.DeviceIdType.MESH
NT = (((1,), (1,)), ((), ()))
ROWS = 256
CLIPS = 32
WIDE = 64
IDS = 16
PIECES = 4


def dot_nt(a, b):
    return lax.dot_general(a, b, NT, preferred_element_type=jnp.float32)


def inverse_root(n):
    r = lax.rsqrt(n)
    return r * (1.5 - 0.5 * n * r * r)


def kernel(
    acts, grads, in_t, out_t, tokens, out,
    abuf, gbuf, ibuf, obuf, blocks, pairs, pool_r, pool_c, scale_r, scale_c,
    held, part, near, half, far,
    load_sem, send1, recv1, send2, recv2, send3, recv3,
    counts, counts_sem, plane_in, other_in, edge_in, next_in, edge_two, two_in,
):
    clip, layer = lax.axis_index("clip"), lax.axis_index("layer")
    z, x, core = clip // 8, (clip // 2) % 4, clip % 2
    y, zh = layer // 4, layer % 4

    def at(clip_bits, layer_bits):
        return (jnp.bitwise_xor(clip, clip_bits), jnp.bitwise_xor(layer, layer_bits))

    token_load = pltpu.make_async_copy(tokens, counts, counts_sem)
    token_load.start()
    loads = [
        pltpu.make_async_copy(in_t.at[0], ibuf, load_sem.at[0]),
        pltpu.make_async_copy(out_t.at[0], obuf, load_sem.at[1]),
    ]
    step = ROWS // PIECES
    for i in range(PIECES):
        rows = pl.ds(i * step, step)
        loads.append(pltpu.make_async_copy(acts.at[0, rows], abuf.at[rows], load_sem.at[2 + 2 * i]))
        loads.append(pltpu.make_async_copy(grads.at[0, rows], gbuf.at[rows], load_sem.at[3 + 2 * i]))
    for load in loads:
        load.start()

    peers = [(8 * d, 0) for d in range(1, 4)]
    peers += [(d, 0) for d in (1, 2, 4, 6)]
    peers += [(0, 4 * d) for d in range(1, 4)]
    low, high = z == 0, z == 3
    edge = jnp.logical_or(low, high)
    on_edge = jnp.where(edge, 1, 0)
    across = (jnp.bitwise_xor(clip, 24), y * 4 + lax.rem(zh + jnp.where(high, 1, 3), 4))
    barrier = pltpu.get_barrier_semaphore()

    def tell(sem, device):
        pl.semaphore_signal(sem, inc=1, device_id=device, device_id_type=MESH)

    for bits in peers:
        tell(barrier, at(*bits))

    @pl.when(edge)
    def _():
        tell(barrier, across)

    place = lax.broadcasted_iota(jnp.int32, (IDS, 128), 0) * 128 + lax.broadcasted_iota(
        jnp.int32, (IDS, 128), 1
    )
    owner = jnp.zeros((IDS, 128), jnp.int32)
    end = jnp.int32(0)
    token_load.wait()
    for c in range(CLIPS - 1):
        end = end + counts[c]
        owner = owner + jnp.where(place >= end, 1, 0)
    blocks[0, ROWS:, :] = owner.astype(jnp.float32).astype(jnp.bfloat16)

    loads[0].wait()
    loads[1].wait()
    for i in range(PIECES):
        rows = pl.ds(i * step, step)
        loads[2 + 2 * i].wait()
        loads[3 + 2 * i].wait()
        v = dot_nt(abuf[rows, :], ibuf[...])
        u = dot_nt(gbuf[rows, :], obuf[...])
        blocks[0, rows, :] = jnp.concatenate([u, v], axis=1).astype(jnp.bfloat16)

    pl.semaphore_wait(barrier, len(peers) + on_edge)

    def send_block(src, slot, bits):
        copy = pltpu.make_async_remote_copy(
            src_ref=blocks.at[src], dst_ref=blocks.at[slot], send_sem=send1.at[slot],
            recv_sem=recv1.at[slot], device_id=at(bits, 0), device_id_type=MESH,
        )
        copy.start()
        return copy

    sends = [send_block(0, 1, 1)]
    for d in (1, 3, 2):
        sends.append(send_block(0, 2 * d, 2 * d))
        sends.append(send_block(0, 7 + d, 8 * d))

    for d in (2, 4, 6):
        tell(plane_in, at(d, 0))

    @pl.when(edge)
    def _():
        tell(edge_in, across)

    def relay_one():
        @pl.when(edge)
        def _():
            pl.semaphore_wait(edge_in, 1)
            for d in range(1, 4):
                tell(next_in, at(8 * d, 0))

    def relay_two():
        pl.semaphore_wait(next_in, 2 - on_edge)

        @pl.when(high)
        def _():
            tell(edge_two, across)

    def relay_three():
        @pl.when(low)
        def _():
            pl.semaphore_wait(edge_two, 1)
            for d in range(1, 4):
                tell(two_in, at(8 * d, 0))

    def relay_four():
        @pl.when(jnp.logical_not(low))
        def _():
            pl.semaphore_wait(two_in, 1)

    def block_arrives(slot):
        pltpu.make_async_remote_copy(
            src_ref=blocks.at[0], dst_ref=blocks.at[slot], send_sem=send1.at[slot],
            recv_sem=recv1.at[slot], device_id=at(1, 0), device_id_type=MESH,
        ).wait_recv()

    lane = lax.broadcasted_iota(jnp.int32, (1, 128), 1)
    group = lane // CLIPS

    def by_group(pieces):
        out = pieces[0]
        for g in range(1, 4):
            out = jnp.where(group == g, pieces[g], out)
        return out

    def hot_ids(slot, which):
        ids = blocks[slot, ROWS:, :].astype(jnp.float32)
        halves = [jnp.where(which == ids[i : i + 1, :], 1.0, 0.0) for i in range(2)]
        return jnp.concatenate(halves, axis=1)

    def place_of(own, k):
        return own if k == 0 else (4 - k) - jnp.where(own >= 4 - k, 1, 0)

    def bits_of(own, k):
        return 0 if k == 0 else jnp.bitwise_xor(own, place_of(own, k))

    def row_slot(kx, i):
        return 2 * bits_of(x, kx) + i

    def take_rows(kx):
        for i in range(2):
            slot = row_slot(kx, i)
            if i:
                block_arrives(slot)
            hot = hot_ids(slot, lax.broadcasted_iota(jnp.int32, (CLIPS, 128), 0).astype(jnp.float32))
            pool_r[kx, i] = hot.astype(jnp.bfloat16)
            scale = inverse_root(jnp.sum(hot, axis=1, keepdims=True))
            scale_r[kx, i] = by_group([scale[8 * g : 8 * g + 8] for g in range(4)])

    def take_cols(kz):
        slot = 0
        if kz:
            slot = 7 + bits_of(z, kz)
            block_arrives(slot)
        cols = blocks[slot, pl.ds(0, ROWS), :]
        pairs[kz, 0:ROWS] = jnp.where(lane < WIDE, cols, jnp.zeros_like(cols))
        pairs[kz, ROWS:] = jnp.where(lane < WIDE, jnp.zeros_like(cols), cols)
        j = lax.broadcasted_iota(jnp.int32, (128, 128), 0)
        which = jnp.where((j // CLIPS) % 2 == kz % 2, j % CLIPS, -1).astype(jnp.float32)
        hot = hot_ids(slot, which).astype(jnp.bfloat16)
        pool_c[kz] = hot
        count = dot_nt(jnp.ones((16, ROWS), jnp.bfloat16), hot)[0:8]
        scale_c[kz] = inverse_root(count + pltpu.roll(count, CLIPS, 1))

    def to_near(kx, i, kz):
        bits, dy = row_slot(kx, i), jnp.bitwise_xor(y, place_of(z, kz))
        slot = bits * 4 + dy
        copy = pltpu.make_async_remote_copy(
            src_ref=part.at[kz, kx, i], dst_ref=near.at[slot], send_sem=send2.at[kz * 8 + kx * 2 + i],
            recv_sem=recv2.at[slot], device_id=at(bits, 4 * dy), device_id_type=MESH,
        )
        return slot, copy

    def pooled_pairs(kx, kz):
        rows = [blocks[row_slot(kx, i), pl.ds(0, ROWS), :] for i in range(2)]
        gram = dot_nt(jnp.concatenate(rows, axis=0), pairs[kz])
        gram = (gram[:, 0:ROWS] * gram[:, ROWS:]).astype(jnp.bfloat16)
        return dot_nt(gram, pool_c[kz])

    def finish(kx, kz, pooled):
        for i in range(2):
            tile = jnp.dot(
                pool_r[kx, i],
                pooled[i * ROWS : (i + 1) * ROWS].astype(jnp.bfloat16),
                preferred_element_type=jnp.float32,
            )
            moved = pltpu.roll(tile, CLIPS, 1)
            for n, k in enumerate((kz - 1, kz)):
                pieces = [(moved if (g + n) % 2 else tile)[8 * g : 8 * g + 8] for g in range(4)]
                part[k, kx, i] = by_group(pieces) * scale_r[kx, i] * scale_c[k]
                slot, copy = to_near(kx, i, k)
                if kx or i:
                    copy.start()
                else:

                    @pl.when(slot != 0)
                    def _():
                        copy.start()

                    @pl.when(slot == 0)
                    def _():
                        near[0] = part[k, 0, 0]

    take_cols(0)
    take_rows(0)
    held[0] = pooled_pairs(0, 0)
    relay_one()
    for kx in (1, 2, 3):
        slot = row_slot(kx, 0)
        block_arrives(slot)
        sends.append(send_block(slot, slot + 1, 1))
    for kx in (1, 2, 3):
        take_rows(kx)
        held[kx] = pooled_pairs(kx, 0)
    relay_two()
    take_cols(1)
    pl.semaphore_wait(plane_in, 3)
    tell(other_in, at(1, 0))
    pl.semaphore_wait(other_in, 1)
    for kx in range(4):
        finish(kx, 1, held[kx] + pooled_pairs(kx, 1))
    relay_three()
    take_cols(2)
    for kx in range(4):
        held[kx] = pooled_pairs(kx, 2)
    take_cols(3)
    for kx in range(4):
        finish(kx, 3, held[kx] + pooled_pairs(kx, 3))
    relay_four()

    def gathered(d, dc):
        bits = 2 * jnp.bitwise_xor(jnp.bitwise_xor(x, zh), d) + dc
        total = jnp.zeros((8, 128), jnp.float32)
        for dy in range(4):
            slot = bits * 4 + dy
            arrival = pltpu.make_async_remote_copy(
                src_ref=part.at[0, 0, 0], dst_ref=near.at[slot], send_sem=send2.at[0],
                recv_sem=recv2.at[slot], device_id=at(1, 0), device_id_type=MESH,
            )
            if dc or dy:
                arrival.wait_recv()
            else:

                @pl.when(slot != 0)
                def _():
                    arrival.wait_recv()

            total = total + near[slot]
        return total

    last = []
    for d in (2, 1, 3):
        for dc in range(2):
            half[d, dc] = gathered(d, dc)
        copy = pltpu.make_async_remote_copy(
            src_ref=half.at[d], dst_ref=far.at[d], send_sem=send3.at[d], recv_sem=recv3.at[d],
            device_id=at(0, d), device_id_type=MESH,
        )
        copy.start()
        last.append(copy)
    total = [gathered(0, dc) for dc in range(2)]
    for copy, d in zip(last, (2, 1, 3), strict=True):
        copy.wait_recv()
        total = [total[dc] + far[d, dc] for dc in range(2)]
    norm = 1.0 / math.sqrt(16 * WIDE * WIDE)
    for side in range(2):
        mine = jnp.where(core == side, total[0], total[1]) * norm
        for g in range(4):
            out[8 * g : 8 * g + 8, CLIPS * side : CLIPS * (side + 1)] = mine[:, CLIPS * g : CLIPS * (g + 1)]

    for copy in sends:
        copy.wait_send()
    for kz in range(4):
        for kx in range(4):
            for i in range(2):
                slot, copy = to_near(kx, i, kz)
                if kx or i:
                    copy.wait_send()
                else:

                    @pl.when(slot != 0)
                    def _():
                        copy.wait_send()

    for copy in last:
        copy.wait_send()


def body(acts, grads, in_factor, out_factor, clip_tokens):
    depth = acts.shape[2]
    bf16, f32 = jnp.bfloat16, jnp.float32
    hbm = pl.BlockSpec(memory_space=pltpu.HBM)
    return pl.pallas_call(
        kernel,
        out_shape=pltpu.VMEM((CLIPS, 64), f32),
        in_specs=[hbm] * 4 + [hbm],
        out_specs=pl.BlockSpec(memory_space=pltpu.VMEM),
        scratch_shapes=[
            pltpu.VMEM((ROWS, depth), bf16),
            pltpu.VMEM((ROWS, depth), bf16),
            pltpu.VMEM((WIDE, depth), bf16),
            pltpu.VMEM((WIDE, depth), bf16),
            pltpu.VMEM((11, ROWS + IDS, 128), bf16),
            pltpu.VMEM((4, 2 * ROWS, 128), bf16),
            pltpu.VMEM((4, 2, CLIPS, ROWS), bf16),
            pltpu.VMEM((4, 128, ROWS), bf16),
            pltpu.VMEM((4, 2, 8, 128), f32),
            pltpu.VMEM((4, 8, 128), f32),
            pltpu.VMEM((4, 2 * ROWS, 128), f32),
            pltpu.VMEM((4, 4, 2, 8, 128), f32),
            pltpu.VMEM((32, 8, 128), f32),
            pltpu.VMEM((4, 2, 8, 128), f32),
            pltpu.VMEM((4, 2, 8, 128), f32),
            pltpu.SemaphoreType.DMA((2 + 2 * PIECES,)),
            pltpu.SemaphoreType.DMA((11,)),
            pltpu.SemaphoreType.DMA((11,)),
            pltpu.SemaphoreType.DMA((32,)),
            pltpu.SemaphoreType.DMA((32,)),
            pltpu.SemaphoreType.DMA((4,)),
            pltpu.SemaphoreType.DMA((4,)),
        ]
        + [pltpu.SMEM((CLIPS,), jnp.int32), pltpu.SemaphoreType.DMA(())]
        + [pltpu.SemaphoreType.REGULAR] * 6,
        compiler_params=pltpu.CompilerParams(
            collective_id=0, has_side_effects=True, vmem_limit_bytes=60 * 1024 * 1024
        ),
        cost_estimate=pl.CostEstimate(flops=10**9, bytes_accessed=7 * 10**6, transcendentals=0),
        name="similarity",
    )(
        acts,
        grads,
        jnp.swapaxes(in_factor, 1, 2),
        jnp.swapaxes(out_factor, 1, 2),
        clip_tokens,
    )


def solution(mesh):
    return jax.shard_map(
        body,
        mesh=mesh,
        in_specs=(
            P("layer", "clip", None),
            P("layer", "clip", None),
            P("layer", None, None),
            P("layer", None, None),
            P("clip"),
        ),
        out_specs=P("clip", "layer"),
        check_vma=False,
    )
```

time: 43.7 us -> 42.3 us (0.968)
  the two profiles are of different devices: /device:TPU:30 before, /device:TPU:34 now
where the time goes in v2:
time: 42.3 us; the launch traced here: 42.2 us
  Pallas kernels  41.5 us (98%)
  local copies, waits for them, and re-layouts  0.61 us (1%)
    pallas_call x1, Pallas kernels, body(): pl.pallas_call(kernel, out_shape=pltpu.VMEM((CLIPS, 64), f32), in_specs=[...  41.5 us

profile of v2, /device:TPU:34, one launch (start us, length us, event | category | flops | bytes accessed | tf_op | source)
XLA Modules:
  0.0 42.2 jit_solution(16314820720126590411)
XLA Ops:
  0.0 41.5 %similarity.1 = f32[32,64]{1,0:T(8,128)S(1)} custom-call(bf16[1,256,5120]{2,1,0:T(8,128)(2,1)} %acts.1, bf16[1,256,5120]{2,1,0:T(8,128)(2,1)} %grads.1, bf16[1,64,5120]{2,1,0:T(8,128)(2,1)} %bitcast.2, bf16[1,64,5120]{2,1,0:T(8,128)(2,1)} %bitcast.3, s32[32]{0:T(128)} %tokens.1), custom_call_target="tpu_custom_call" | custom-call | flops 1000000000 | bytes 7000000 | tf_op jit(solution)/shard_map/similarity/pallas_call | solution.py:327
  41.5 0.6 %copy.7 = f32[32,64]{1,0:T(8,128)} copy(f32[32,64]{1,0:T(8,128)S(1)} %similarity.1) | data formatting | bytes 16384

commit v3 on v2

--- a/solution.py
+++ b/solution.py
@@ -30,12 +30,23 @@
     acts, grads, in_t, out_t, tokens, out,
     abuf, gbuf, ibuf, obuf, blocks, pairs, pool_r, pool_c, scale_r, scale_c,
     held, part, near, half, far,
-    load_sem, send1, recv1, send2, recv2, send3, recv3,
-    counts, counts_sem, plane_in, other_in, edge_in, next_in, edge_two, two_in,
+    load_sem, send1, recv1, send2, recv2, send3, recv3, recv4,
+    counts, counts_sem, plane_in, other_in, run_in, edge_in, next_in, edge_two, two_in,
 ):
     clip, layer = lax.axis_index("clip"), lax.axis_index("layer")
     z, x, core = clip // 8, (clip // 2) % 4, clip % 2
     y, zh = layer // 4, layer % 4
+
+    turn = jnp.where(zh >= 2, z, 3 - z)
+
+    def by_turn(values):
+        return sum(jnp.where(turn == n, value, 0) for n, value in enumerate(values))
+
+    takes = (by_turn((3, 3, 2, 1)), by_turn((0, 1, 0, 2)))
+    gives = (by_turn((1, 2, 3, 3)), by_turn((2, 0, 1, 0)))
+    takes_two, gives_two = turn % 2 == 1, turn % 2 == 0
+    apart = jnp.bitwise_xor(y, z)
+    mine = (apart == 0) | (apart == takes[0]) | (takes_two & (apart == takes[1]))
 
     def at(clip_bits, layer_bits):
         return (jnp.bitwise_xor(clip, clip_bits), jnp.bitwise_xor(layer, layer_bits))
@@ -104,13 +115,25 @@
         copy.start()
         return copy
 
-    sends = [send_block(0, 1, 1)]
-    for d in (1, 3, 2):
-        sends.append(send_block(0, 2 * d, 2 * d))
-        sends.append(send_block(0, 7 + d, 8 * d))
-
-    for d in (2, 4, 6):
-        tell(plane_in, at(d, 0))
+    def column_send(n):
+        return pltpu.make_async_remote_copy(
+            src_ref=blocks.at[0], dst_ref=blocks.at[7 + gives[n]], send_sem=send1.at[8 + n],
+            recv_sem=recv1.at[7 + gives[n]], device_id=at(8 * gives[n], 0), device_id_type=MESH,
+        )
+
+    sends = [send_block(0, 1, 1), send_block(0, 2, 2)]
+    column_send(0).start()
+    sends.append(send_block(0, 6, 6))
+
+    @pl.when(gives_two)
+    def _():
+        column_send(1).start()
+
+    sends.append(send_block(0, 4, 4))
+
+    for d in range(1, 4):
+        tell(plane_in, at(2 * d, 0))
+        tell(run_in, at(8 * d, 0))
 
     @pl.when(edge)
     def _():
@@ -162,14 +185,14 @@
         halves = [jnp.where(which == ids[i : i + 1, :], 1.0, 0.0) for i in range(2)]
         return jnp.concatenate(halves, axis=1)
 
-    def place_of(own, k):
-        return own if k == 0 else (4 - k) - jnp.where(own >= 4 - k, 1, 0)
-
-    def bits_of(own, k):
-        return 0 if k == 0 else jnp.bitwise_xor(own, place_of(own, k))
+    def place_up(own, k):
+        return own if k == 0 else (k - 1) + jnp.where(own <= k - 1, 1, 0)
+
+    def bits_x(k):
+        return 0 if k == 0 else jnp.bitwise_xor(x, place_up(x, k))
 
     def row_slot(kx, i):
-        return 2 * bits_of(x, kx) + i
+        return 2 * bits_x(kx) + i
 
     def take_rows(kx):
         for i in range(2):
@@ -184,7 +207,7 @@
     def take_cols(kz):
         slot = 0
         if kz:
-            slot = 7 + bits_of(z, kz)
+            slot = 7 + takes[kz - 1]
             block_arrives(slot)
         cols = blocks[slot, pl.ds(0, ROWS), :]
         pairs[kz, 0:ROWS] = jnp.where(lane < WIDE, cols, jnp.zeros_like(cols))
@@ -197,13 +220,19 @@
         scale_c[kz] = inverse_root(count + pltpu.roll(count, CLIPS, 1))
 
     def to_near(kx, i, kz):
-        bits, dy = row_slot(kx, i), jnp.bitwise_xor(y, place_of(z, kz))
-        slot = bits * 4 + dy
+        bits = row_slot(kx, i)
+        dy = jnp.bitwise_xor(apart, takes[kz - 1]) if kz else apart
         copy = pltpu.make_async_remote_copy(
-            src_ref=part.at[kz, kx, i], dst_ref=near.at[slot], send_sem=send2.at[kz * 8 + kx * 2 + i],
-            recv_sem=recv2.at[slot], device_id=at(bits, 4 * dy), device_id_type=MESH,
-        )
-        return slot, copy
+            src_ref=part.at[kz, bits], dst_ref=near.at[dy, bits], send_sem=send2.at[kz * 8 + kx * 2 + i],
+            recv_sem=recv2.at[dy * 8 + bits], device_id=at(bits, 4 * dy), device_id_type=MESH,
+        )
+        return dy * 8 + bits, copy
+
+    def to_other_run(kz):
+        return pltpu.make_async_remote_copy(
+            src_ref=part.at[kz], dst_ref=near.at[apart], send_sem=send2.at[24 + kz],
+            recv_sem=recv4.at[apart], device_id=at(8 * takes[kz - 1], 4 * apart), device_id_type=MESH,
+        )
 
     def pooled_pairs(kx, kz):
         rows = [blocks[row_slot(kx, i), pl.ds(0, ROWS), :] for i in range(2)]
@@ -211,7 +240,7 @@
         gram = (gram[:, 0:ROWS] * gram[:, ROWS:]).astype(jnp.bfloat16)
         return dot_nt(gram, pool_c[kz])
 
-    def finish(kx, kz, pooled):
+    def finish(kx, kzs, pooled):
         for i in range(2):
             tile = jnp.dot(
                 pool_r[kx, i],
@@ -219,9 +248,9 @@
                 preferred_element_type=jnp.float32,
             )
             moved = pltpu.roll(tile, CLIPS, 1)
-            for n, k in enumerate((kz - 1, kz)):
+            for n, k in enumerate(kzs):
                 pieces = [(moved if (g + n) % 2 else tile)[8 * g : 8 * g + 8] for g in range(4)]
-                part[k, kx, i] = by_group(pieces) * scale_r[kx, i] * scale_c[k]
+                part[k, row_slot(kx, i)] = by_group(pieces) * scale_r[kx, i] * scale_c[k]
                 slot, copy = to_near(kx, i, k)
                 if kx or i:
                     copy.start()
@@ -233,7 +262,7 @@
 
                     @pl.when(slot == 0)
                     def _():
-                        near[0] = part[k, 0, 0]
+                        near[0, 0] = part[k, 0]
 
     take_cols(0)
     take_rows(0)
@@ -247,39 +276,48 @@
         take_rows(kx)
         held[kx] = pooled_pairs(kx, 0)
     relay_two()
-    take_cols(1)
     pl.semaphore_wait(plane_in, 3)
     tell(other_in, at(1, 0))
+    pl.semaphore_wait(run_in, 3)
+    take_cols(1)
     pl.semaphore_wait(other_in, 1)
     for kx in range(4):
-        finish(kx, 1, held[kx] + pooled_pairs(kx, 1))
+        finish(kx, (0, 1), held[kx] + pooled_pairs(kx, 1))
+    to_other_run(1).start()
     relay_three()
-    take_cols(2)
-    for kx in range(4):
-        held[kx] = pooled_pairs(kx, 2)
-    take_cols(3)
-    for kx in range(4):
-        finish(kx, 3, held[kx] + pooled_pairs(kx, 3))
+
+    @pl.when(takes_two)
+    def _():
+        take_cols(2)
+        for kx in range(4):
+            finish(kx, (2,), pooled_pairs(kx, 2))
+        to_other_run(2).start()
+
     relay_four()
+
+    @pl.when(jnp.logical_not(mine))
+    def _():
+        for dy in range(4):
+            pltpu.make_async_remote_copy(
+                src_ref=part.at[0], dst_ref=near.at[dy], send_sem=send2.at[25],
+                recv_sem=recv4.at[dy], device_id=at(1, 0), device_id_type=MESH,
+            ).wait_recv()
 
     def gathered(d, dc):
         bits = 2 * jnp.bitwise_xor(jnp.bitwise_xor(x, zh), d) + dc
         total = jnp.zeros((8, 128), jnp.float32)
         for dy in range(4):
-            slot = bits * 4 + dy
+            slot = dy * 8 + bits
             arrival = pltpu.make_async_remote_copy(
-                src_ref=part.at[0, 0, 0], dst_ref=near.at[slot], send_sem=send2.at[0],
+                src_ref=part.at[0, 0], dst_ref=near.at[dy, bits], send_sem=send2.at[0],
                 recv_sem=recv2.at[slot], device_id=at(1, 0), device_id_type=MESH,
             )
-            if dc or dy:
+
+            @pl.when(mine & (slot != 0))
+            def _():
                 arrival.wait_recv()
-            else:
-
-                @pl.when(slot != 0)
-                def _():
-                    arrival.wait_recv()
-
-            total = total + near[slot]
+
+            total = total + near[dy, bits]
         return total
 
     last = []
@@ -293,18 +331,33 @@
         copy.start()
         last.append(copy)
     total = [gathered(0, dc) for dc in range(2)]
-    for copy, d in zip(last, (2, 1, 3), strict=True):
+    for copy in last:
         copy.wait_recv()
-        total = [total[dc] + far[d, dc] for dc in range(2)]
     norm = 1.0 / math.sqrt(16 * WIDE * WIDE)
     for side in range(2):
-        mine = jnp.where(core == side, total[0], total[1]) * norm
-        for g in range(4):
-            out[8 * g : 8 * g + 8, CLIPS * side : CLIPS * (side + 1)] = mine[:, CLIPS * g : CLIPS * (g + 1)]
+        here, there = (
+            jnp.where(core == side, pair[0], pair[1]) * norm
+            for pair in ([total[dc] + far[1, dc] for dc in range(2)], [far[2, dc] + far[3, dc] for dc in range(2)])
+        )
+        straight = jnp.where(mine, here, there) + jnp.where(apart == 0, there, 0.0)
+        crossed = jnp.where(apart == 0, 0.0, jnp.where(mine, there, here))
+        straight, crossed = (
+            jnp.concatenate([packed[:, CLIPS * g : CLIPS * (g + 1)] for g in range(4)], axis=0)
+            for packed in (straight, crossed)
+        )
+        crossed = jnp.concatenate([crossed, jnp.zeros((CLIPS, 128 - CLIPS), jnp.float32)], axis=1)
+        crossed = jnp.concatenate([crossed, jnp.zeros((128 - CLIPS, 128), jnp.float32)], axis=0)
+        out[:, CLIPS * side : CLIPS * (side + 1)] = straight + crossed.T[0:CLIPS, 0:CLIPS]
 
     for copy in sends:
         copy.wait_send()
-    for kz in range(4):
+    column_send(0).wait_send()
+
+    @pl.when(gives_two)
+    def _():
+        column_send(1).wait_send()
+
+    def near_sent(kz):
         for kx in range(4):
             for i in range(2):
                 slot, copy = to_near(kx, i, kz)
@@ -315,6 +368,16 @@
                     @pl.when(slot != 0)
                     def _():
                         copy.wait_send()
+
+        if kz:
+            to_other_run(kz).wait_send()
+
+    near_sent(0)
+    near_sent(1)
+
+    @pl.when(takes_two)
+    def _():
+        near_sent(2)
 
     for copy in last:
         copy.wait_send()
@@ -341,8 +404,8 @@
             pltpu.VMEM((4, 2, 8, 128), f32),
             pltpu.VMEM((4, 8, 128), f32),
             pltpu.VMEM((4, 2 * ROWS, 128), f32),
-            pltpu.VMEM((4, 4, 2, 8, 128), f32),
-            pltpu.VMEM((32, 8, 128), f32),
+            pltpu.VMEM((3, 8, 8, 128), f32),
+            pltpu.VMEM((4, 8, 8, 128), f32),
             pltpu.VMEM((4, 2, 8, 128), f32),
             pltpu.VMEM((4, 2, 8, 128), f32),
             pltpu.SemaphoreType.DMA((2 + 2 * PIECES,)),
@@ -352,9 +415,10 @@
             pltpu.SemaphoreType.DMA((32,)),
             pltpu.SemaphoreType.DMA((4,)),
             pltpu.SemaphoreType.DMA((4,)),
+            pltpu.SemaphoreType.DMA((4,)),
         ]
         + [pltpu.SMEM((CLIPS,), jnp.int32), pltpu.SemaphoreType.DMA(())]
-        + [pltpu.SemaphoreType.REGULAR] * 6,
+        + [pltpu.SemaphoreType.REGULAR] * 7,
         compiler_params=pltpu.CompilerParams(
             collective_id=0, has_side_effects=True, vmem_limit_bytes=60 * 1024 * 1024
         ),

time: 42.3 us -> 41.8 us (0.988)
  the two profiles are of different devices: /device:TPU:34 before, /device:TPU:8 now
where the time goes in v3:
time: 41.8 us; the launch traced here: 41.7 us
  Pallas kernels  41.1 us (98%)
  local copies, waits for them, and re-layouts  0.61 us (1%)
    pallas_call x1, Pallas kernels, body(): pl.pallas_call(kernel, out_shape=pltpu.VMEM((CLIPS, 64), f32), in_specs=[...  41.1 us

profile of v3, /device:TPU:8, one launch (start us, length us, event | category | flops | bytes accessed | tf_op | source)
XLA Modules:
  0.0 41.7 jit_solution(5971412871792810057)
XLA Ops:
  0.0 41.1 %similarity.1 = f32[32,64]{1,0:T(8,128)S(1)} custom-call(bf16[1,256,5120]{2,1,0:T(8,128)(2,1)} %acts.1, bf16[1,256,5120]{2,1,0:T(8,128)(2,1)} %grads.1, bf16[1,64,5120]{2,1,0:T(8,128)(2,1)} %bitcast.2, bf16[1,64,5120]{2,1,0:T(8,128)(2,1)} %bitcast.3, s32[32]{0:T(128)} %tokens.1), custom_call_target="tpu_custom_call" | custom-call | flops 1000000000 | bytes 7000000 | tf_op jit(solution)/shard_map/similarity/pallas_call | solution.py:390
  41.1 0.6 %copy.7 = f32[32,64]{1,0:T(8,128)} copy(f32[32,64]{1,0:T(8,128)S(1)} %similarity.1) | data formatting | bytes 16384

commit v4 on v3

--- a/solution.py
+++ b/solution.py
@@ -38,15 +38,14 @@
     y, zh = layer // 4, layer % 4
 
     turn = jnp.where(zh >= 2, z, 3 - z)
-
-    def by_turn(values):
-        return sum(jnp.where(turn == n, value, 0) for n, value in enumerate(values))
-
-    takes = (by_turn((3, 3, 2, 1)), by_turn((0, 1, 0, 2)))
-    gives = (by_turn((1, 2, 3, 3)), by_turn((2, 0, 1, 0)))
-    takes_two, gives_two = turn % 2 == 1, turn % 2 == 0
+    odd = turn % 2
+    takes = (jnp.where(turn < 2, 3, 2), 1)
+    gives = (jnp.where(turn < 2, 2, 3), 1)
     apart = jnp.bitwise_xor(y, z)
-    mine = (apart == 0) | (apart == takes[0]) | (takes_two & (apart == takes[1]))
+
+    def straight_from(dx):
+        half = (dx // 2) == odd
+        return (apart == 0) | (apart == takes[0]) | ((apart == 1) & half)
 
     def at(clip_bits, layer_bits):
         return (jnp.bitwise_xor(clip, clip_bits), jnp.bitwise_xor(layer, layer_bits))
@@ -121,16 +120,9 @@
             recv_sem=recv1.at[7 + gives[n]], device_id=at(8 * gives[n], 0), device_id_type=MESH,
         )
 
-    sends = [send_block(0, 1, 1), send_block(0, 2, 2)]
+    sends = [send_block(0, 1, 1), send_block(0, 4, 4), send_block(0, 2, 2), send_block(0, 6, 6)]
     column_send(0).start()
-    sends.append(send_block(0, 6, 6))
-
-    @pl.when(gives_two)
-    def _():
-        column_send(1).start()
-
-    sends.append(send_block(0, 4, 4))
-
+    column_send(1).start()
     for d in range(1, 4):
         tell(plane_in, at(2 * d, 0))
         tell(run_in, at(8 * d, 0))
@@ -185,14 +177,8 @@
         halves = [jnp.where(which == ids[i : i + 1, :], 1.0, 0.0) for i in range(2)]
         return jnp.concatenate(halves, axis=1)
 
-    def place_up(own, k):
-        return own if k == 0 else (k - 1) + jnp.where(own <= k - 1, 1, 0)
-
-    def bits_x(k):
-        return 0 if k == 0 else jnp.bitwise_xor(x, place_up(x, k))
-
     def row_slot(kx, i):
-        return 2 * bits_x(kx) + i
+        return 2 * kx + i
 
     def take_rows(kx):
         for i in range(2):
@@ -228,9 +214,15 @@
         )
         return dy * 8 + bits, copy
 
+    def may_stay(kx, i):
+        return i == 0 and not (isinstance(kx, int) and kx)
+
     def to_other_run(kz):
+        here, there = part.at[kz], near.at[apart]
+        if kz == 2:
+            here, there = part.at[2, pl.ds(4 * odd, 4)], near.at[apart, pl.ds(4 * odd, 4)]
         return pltpu.make_async_remote_copy(
-            src_ref=part.at[kz], dst_ref=near.at[apart], send_sem=send2.at[24 + kz],
+            src_ref=here, dst_ref=there, send_sem=send2.at[24 + kz],
             recv_sem=recv4.at[apart], device_id=at(8 * takes[kz - 1], 4 * apart), device_id_type=MESH,
         )
 
@@ -252,7 +244,7 @@
                 pieces = [(moved if (g + n) % 2 else tile)[8 * g : 8 * g + 8] for g in range(4)]
                 part[k, row_slot(kx, i)] = by_group(pieces) * scale_r[kx, i] * scale_c[k]
                 slot, copy = to_near(kx, i, k)
-                if kx or i:
+                if not may_stay(kx, i):
                     copy.start()
                 else:
 
@@ -268,43 +260,51 @@
     take_rows(0)
     held[0] = pooled_pairs(0, 0)
     relay_one()
-    for kx in (1, 2, 3):
+    for kx in (1, 3, 2):
         slot = row_slot(kx, 0)
         block_arrives(slot)
         sends.append(send_block(slot, slot + 1, 1))
-    for kx in (1, 2, 3):
-        take_rows(kx)
-        held[kx] = pooled_pairs(kx, 0)
-    relay_two()
     pl.semaphore_wait(plane_in, 3)
     tell(other_in, at(1, 0))
-    pl.semaphore_wait(run_in, 3)
+    relay_two()
     take_cols(1)
+    take_cols(2)
     pl.semaphore_wait(other_in, 1)
-    for kx in range(4):
+    for kx in (0, 1, 3, 2):
+        if kx:
+            take_rows(kx)
+            held[kx] = pooled_pairs(kx, 0)
         finish(kx, (0, 1), held[kx] + pooled_pairs(kx, 1))
+        if kx == 1:
+            relay_three()
+        if kx == 3:
+            pl.semaphore_wait(run_in, 3)
     to_other_run(1).start()
-    relay_three()
-
-    @pl.when(takes_two)
-    def _():
-        take_cols(2)
-        for kx in range(4):
-            finish(kx, (2,), pooled_pairs(kx, 2))
-        to_other_run(2).start()
-
+    halves = [jnp.bitwise_xor(n, 3 * odd) for n in range(2)]
+    for kx in halves:
+        finish(kx, (2,), pooled_pairs(kx, 2))
+    to_other_run(2).start()
     relay_four()
 
-    @pl.when(jnp.logical_not(mine))
+    def run_arrives(dy, there):
+        pltpu.make_async_remote_copy(
+            src_ref=there, dst_ref=there, send_sem=send2.at[25],
+            recv_sem=recv4.at[dy], device_id=at(1, 0), device_id_type=MESH,
+        ).wait_recv()
+
+    @pl.when(apart == 1)
     def _():
         for dy in range(4):
-            pltpu.make_async_remote_copy(
-                src_ref=part.at[0], dst_ref=near.at[dy], send_sem=send2.at[25],
-                recv_sem=recv4.at[dy], device_id=at(1, 0), device_id_type=MESH,
-            ).wait_recv()
+            run_arrives(dy, near.at[dy, pl.ds(4 * (1 - odd), 4)])
+
+    @pl.when(jnp.logical_not((apart == 0) | (apart == 1) | (apart == takes[0])))
+    def _():
+        for dy in range(4):
+            run_arrives(dy, near.at[dy])
 
     def gathered(d, dc):
-        bits = 2 * jnp.bitwise_xor(jnp.bitwise_xor(x, zh), d) + dc
+        dx = jnp.bitwise_xor(jnp.bitwise_xor(x, zh), d)
+        bits = 2 * dx + dc
         total = jnp.zeros((8, 128), jnp.float32)
         for dy in range(4):
             slot = dy * 8 + bits
@@ -313,7 +313,7 @@
                 recv_sem=recv2.at[slot], device_id=at(1, 0), device_id_type=MESH,
             )
 
-            @pl.when(mine & (slot != 0))
+            @pl.when(straight_from(dx) & (slot != 0))
             def _():
                 arrival.wait_recv()
 
@@ -334,6 +334,7 @@
     for copy in last:
         copy.wait_recv()
     norm = 1.0 / math.sqrt(16 * WIDE * WIDE)
+    mine = straight_from(jnp.bitwise_xor(x, zh))
     for side in range(2):
         here, there = (
             jnp.where(core == side, pair[0], pair[1]) * norm
@@ -353,32 +354,26 @@
         copy.wait_send()
     column_send(0).wait_send()
 
-    @pl.when(gives_two)
-    def _():
-        column_send(1).wait_send()
-
-    def near_sent(kz):
-        for kx in range(4):
-            for i in range(2):
-                slot, copy = to_near(kx, i, kz)
-                if kx or i:
+    column_send(1).wait_send()
+
+    def near_sent(kx, kz):
+        for i in range(2):
+            slot, copy = to_near(kx, i, kz)
+            if not may_stay(kx, i):
+                copy.wait_send()
+            else:
+
+                @pl.when(slot != 0)
+                def _():
                     copy.wait_send()
-                else:
-
-                    @pl.when(slot != 0)
-                    def _():
-                        copy.wait_send()
-
-        if kz:
-            to_other_run(kz).wait_send()
-
-    near_sent(0)
-    near_sent(1)
-
-    @pl.when(takes_two)
-    def _():
-        near_sent(2)
-
+
+    for kx in range(4):
+        for kz in range(2):
+            near_sent(kx, kz)
+    for kx in halves:
+        near_sent(kx, 2)
+    for kz in (1, 2):
+        to_other_run(kz).wait_send()
     for copy in last:
         copy.wait_send()
 

time: 41.8 us -> 39.5 us (0.945)
  the two profiles are of different devices: /device:TPU:8 before, /device:TPU:32 now
where the time goes in v4:
time: 39.5 us; the launch traced here: 39.3 us
  Pallas kernels  38.7 us (98%)
  local copies, waits for them, and re-layouts  0.61 us (2%)
    pallas_call x1, Pallas kernels, body(): pl.pallas_call(kernel, out_shape=pltpu.VMEM((CLIPS, 64), f32), in_specs=[...  38.7 us

profile of v4, /device:TPU:32, one launch (start us, length us, event | category | flops | bytes accessed | tf_op | source)
XLA Modules:
  0.0 39.3 jit_solution(16194722069342709614)
XLA Ops:
  0.0 38.7 %similarity.1 = f32[32,64]{1,0:T(8,128)S(1)} custom-call(bf16[1,256,5120]{2,1,0:T(8,128)(2,1)} %acts.1, bf16[1,256,5120]{2,1,0:T(8,128)(2,1)} %grads.1, bf16[1,64,5120]{2,1,0:T(8,128)(2,1)} %bitcast.2, bf16[1,64,5120]{2,1,0:T(8,128)(2,1)} %bitcast.3, s32[32]{0:T(128)} %tokens.1), custom_call_target="tpu_custom_call" | custom-call | flops 1000000000 | bytes 7000000 | tf_op jit(solution)/shard_map/similarity/pallas_call | solution.py:385
  38.7 0.6 %copy.7 = f32[32,64]{1,0:T(8,128)} copy(f32[32,64]{1,0:T(8,128)S(1)} %similarity.1) | data formatting | bytes 16384

commit v5 on v4

--- a/solution.py
+++ b/solution.py
@@ -210,7 +210,7 @@
         dy = jnp.bitwise_xor(apart, takes[kz - 1]) if kz else apart
         copy = pltpu.make_async_remote_copy(
             src_ref=part.at[kz, bits], dst_ref=near.at[dy, bits], send_sem=send2.at[kz * 8 + kx * 2 + i],
-            recv_sem=recv2.at[dy * 8 + bits], device_id=at(bits, 4 * dy), device_id_type=MESH,
+            recv_sem=recv2.at[bits // 2], device_id=at(bits, 4 * dy), device_id_type=MESH,
         )
         return dy * 8 + bits, copy
 
@@ -223,7 +223,7 @@
             here, there = part.at[2, pl.ds(4 * odd, 4)], near.at[apart, pl.ds(4 * odd, 4)]
         return pltpu.make_async_remote_copy(
             src_ref=here, dst_ref=there, send_sem=send2.at[24 + kz],
-            recv_sem=recv4.at[apart], device_id=at(8 * takes[kz - 1], 4 * apart), device_id_type=MESH,
+            recv_sem=recv4, device_id=at(8 * takes[kz - 1], 4 * apart), device_id_type=MESH,
         )
 
     def pooled_pairs(kx, kz):
@@ -254,7 +254,7 @@
 
                     @pl.when(slot == 0)
                     def _():
-                        near[0, 0] = part[k, 0]
+                        pltpu.make_async_copy(part.at[k, 0], near.at[0, 0], recv2.at[0]).start()
 
     take_cols(0)
     take_rows(0)
@@ -286,70 +286,43 @@
     to_other_run(2).start()
     relay_four()
 
-    def run_arrives(dy, there):
+    def run_arrives(there):
         pltpu.make_async_remote_copy(
             src_ref=there, dst_ref=there, send_sem=send2.at[25],
-            recv_sem=recv4.at[dy], device_id=at(1, 0), device_id_type=MESH,
+            recv_sem=recv4, device_id=at(1, 0), device_id_type=MESH,
         ).wait_recv()
 
     @pl.when(apart == 1)
     def _():
-        for dy in range(4):
-            run_arrives(dy, near.at[dy, pl.ds(4 * (1 - odd), 4)])
+        run_arrives(near.at[:, pl.ds(4 * (1 - odd), 4)])
 
     @pl.when(jnp.logical_not((apart == 0) | (apart == 1) | (apart == takes[0])))
     def _():
-        for dy in range(4):
-            run_arrives(dy, near.at[dy])
-
-    def gathered(d, dc):
+        run_arrives(near)
+
+    def gathered(d):
         dx = jnp.bitwise_xor(jnp.bitwise_xor(x, zh), d)
-        bits = 2 * dx + dc
-        total = jnp.zeros((8, 128), jnp.float32)
-        for dy in range(4):
-            slot = dy * 8 + bits
-            arrival = pltpu.make_async_remote_copy(
-                src_ref=part.at[0, 0], dst_ref=near.at[dy, bits], send_sem=send2.at[0],
-                recv_sem=recv2.at[slot], device_id=at(1, 0), device_id_type=MESH,
-            )
-
-            @pl.when(straight_from(dx) & (slot != 0))
-            def _():
-                arrival.wait_recv()
-
-            total = total + near[dy, bits]
-        return total
+        both = pl.ds(2 * dx, 2)
+
+        @pl.when(straight_from(dx))
+        def _():
+            pltpu.make_async_remote_copy(
+                src_ref=near.at[:, both], dst_ref=near.at[:, both], send_sem=send2.at[0],
+                recv_sem=recv2.at[dx], device_id=at(1, 0), device_id_type=MESH,
+            ).wait_recv()
+
+        return near[0, both] + near[1, both] + near[2, both] + near[3, both]
 
     last = []
     for d in (2, 1, 3):
-        for dc in range(2):
-            half[d, dc] = gathered(d, dc)
+        half[d] = gathered(d)
         copy = pltpu.make_async_remote_copy(
             src_ref=half.at[d], dst_ref=far.at[d], send_sem=send3.at[d], recv_sem=recv3.at[d],
             device_id=at(0, d), device_id_type=MESH,
         )
         copy.start()
         last.append(copy)
-    total = [gathered(0, dc) for dc in range(2)]
-    for copy in last:
-        copy.wait_recv()
-    norm = 1.0 / math.sqrt(16 * WIDE * WIDE)
-    mine = straight_from(jnp.bitwise_xor(x, zh))
-    for side in range(2):
-        here, there = (
-            jnp.where(core == side, pair[0], pair[1]) * norm
-            for pair in ([total[dc] + far[1, dc] for dc in range(2)], [far[2, dc] + far[3, dc] for dc in range(2)])
-        )
-        straight = jnp.where(mine, here, there) + jnp.where(apart == 0, there, 0.0)
-        crossed = jnp.where(apart == 0, 0.0, jnp.where(mine, there, here))
-        straight, crossed = (
-            jnp.concatenate([packed[:, CLIPS * g : CLIPS * (g + 1)] for g in range(4)], axis=0)
-            for packed in (straight, crossed)
-        )
-        crossed = jnp.concatenate([crossed, jnp.zeros((CLIPS, 128 - CLIPS), jnp.float32)], axis=1)
-        crossed = jnp.concatenate([crossed, jnp.zeros((128 - CLIPS, 128), jnp.float32)], axis=0)
-        out[:, CLIPS * side : CLIPS * (side + 1)] = straight + crossed.T[0:CLIPS, 0:CLIPS]
-
+    total = gathered(0)
     for copy in sends:
         copy.wait_send()
     column_send(0).wait_send()
@@ -376,6 +349,25 @@
         to_other_run(kz).wait_send()
     for copy in last:
         copy.wait_send()
+
+    for copy in last:
+        copy.wait_recv()
+    norm = 1.0 / math.sqrt(16 * WIDE * WIDE)
+    mine = straight_from(jnp.bitwise_xor(x, zh))
+    for side in range(2):
+        here, there = (
+            jnp.where(core == side, pair[0], pair[1]) * norm
+            for pair in ([total[dc] + far[1, dc] for dc in range(2)], [far[2, dc] + far[3, dc] for dc in range(2)])
+        )
+        straight = jnp.where(mine, here, there) + jnp.where(apart == 0, there, 0.0)
+        crossed = jnp.where(apart == 0, 0.0, jnp.where(mine, there, here))
+        straight, crossed = (
+            jnp.concatenate([packed[:, CLIPS * g : CLIPS * (g + 1)] for g in range(4)], axis=0)
+            for packed in (straight, crossed)
+        )
+        crossed = jnp.concatenate([crossed, jnp.zeros((CLIPS, 128 - CLIPS), jnp.float32)], axis=1)
+        crossed = jnp.concatenate([crossed, jnp.zeros((128 - CLIPS, 128), jnp.float32)], axis=0)
+        out[:, CLIPS * side : CLIPS * (side + 1)] = straight + crossed.T[0:CLIPS, 0:CLIPS]
 
 
 def body(acts, grads, in_factor, out_factor, clip_tokens):
@@ -407,10 +399,10 @@
             pltpu.SemaphoreType.DMA((11,)),
             pltpu.SemaphoreType.DMA((11,)),
             pltpu.SemaphoreType.DMA((32,)),
-            pltpu.SemaphoreType.DMA((32,)),
             pltpu.SemaphoreType.DMA((4,)),
             pltpu.SemaphoreType.DMA((4,)),
             pltpu.SemaphoreType.DMA((4,)),
+            pltpu.SemaphoreType.DMA(()),
         ]
         + [pltpu.SMEM((CLIPS,), jnp.int32), pltpu.SemaphoreType.DMA(())]
         + [pltpu.SemaphoreType.REGULAR] * 7,

time: 39.5 us -> 39.1 us (0.990)
  no operation moved by 1% of the time
where the time goes in v5:
time: 39.1 us; the launch traced here: 39 us
  Pallas kernels  38.4 us (98%)
  local copies, waits for them, and re-layouts  0.61 us (2%)
    pallas_call x1, Pallas kernels, body(): pl.pallas_call(kernel, out_shape=pltpu.VMEM((CLIPS, 64), f32), in_specs=[...  38.4 us

profile of v5, /device:TPU:32, one launch (start us, length us, event | category | flops | bytes accessed | tf_op | source)
XLA Modules:
  0.0 39.0 jit_solution(1157805069408419181)
XLA Ops:
  0.0 38.4 %similarity.1 = f32[32,64]{1,0:T(8,128)S(1)} custom-call(bf16[1,256,5120]{2,1,0:T(8,128)(2,1)} %acts.1, bf16[1,256,5120]{2,1,0:T(8,128)(2,1)} %grads.1, bf16[1,64,5120]{2,1,0:T(8,128)(2,1)} %bitcast.2, bf16[1,64,5120]{2,1,0:T(8,128)(2,1)} %bitcast.3, s32[32]{0:T(128)} %tokens.1), custom_call_target="tpu_custom_call" | custom-call | flops 1000000000 | bytes 7000000 | tf_op jit(solution)/shard_map/similarity/pallas_call | solution.py:377
  38.4 0.6 %copy.7 = f32[32,64]{1,0:T(8,128)} copy(f32[32,64]{1,0:T(8,128)S(1)} %similarity.1) | data formatting | bytes 16384

commit v6 on v5

--- a/solution.py
+++ b/solution.py
@@ -183,7 +183,7 @@
     def take_rows(kx):
         for i in range(2):
             slot = row_slot(kx, i)
-            if i:
+            if i and not kx:
                 block_arrives(slot)
             hot = hot_ids(slot, lax.broadcasted_iota(jnp.int32, (CLIPS, 128), 0).astype(jnp.float32))
             pool_r[kx, i] = hot.astype(jnp.bfloat16)
@@ -272,8 +272,9 @@
     pl.semaphore_wait(other_in, 1)
     for kx in (0, 1, 3, 2):
         if kx:
+            block_arrives(row_slot(kx, 1))
+            held[kx] = pooled_pairs(kx, 0)
             take_rows(kx)
-            held[kx] = pooled_pairs(kx, 0)
         finish(kx, (0, 1), held[kx] + pooled_pairs(kx, 1))
         if kx == 1:
             relay_three()

time: 39.1 us -> 38.8 us (level)
  no operation moved by 1% of the time
where the time goes in v6:
time: 38.8 us; the launch traced here: 38.7 us
  Pallas kernels  38.1 us (98%)
  local copies, waits for them, and re-layouts  0.61 us (2%)
    pallas_call x1, Pallas kernels, body(): pl.pallas_call(kernel, out_shape=pltpu.VMEM((CLIPS, 64), f32), in_specs=[...  38.1 us

profile of v6, /device:TPU:32, one launch (start us, length us, event | category | flops | bytes accessed | tf_op | source)
XLA Modules:
  0.0 38.7 jit_solution(248943831379310594)
XLA Ops:
  0.0 38.1 %similarity.1 = f32[32,64]{1,0:T(8,128)S(1)} custom-call(bf16[1,256,5120]{2,1,0:T(8,128)(2,1)} %acts.1, bf16[1,256,5120]{2,1,0:T(8,128)(2,1)} %grads.1, bf16[1,64,5120]{2,1,0:T(8,128)(2,1)} %bitcast.2, bf16[1,64,5120]{2,1,0:T(8,128)(2,1)} %bitcast.3, s32[32]{0:T(128)} %tokens.1), custom_call_target="tpu_custom_call" | custom-call | flops 1000000000 | bytes 7000000 | tf_op jit(solution)/shard_map/similarity/pallas_call | solution.py:378
  38.1 0.6 %copy.7 = f32[32,64]{1,0:T(8,128)} copy(f32[32,64]{1,0:T(8,128)S(1)} %similarity.1) | data formatting | bytes 16384
